TPU v7x, 256 devices: a whole 4x4x8 slice. The times are simulated.
256 devices in a mesh: wave: 64 (over x, z, core), fld: 4 (over y).
Axes of the slice: x: 4, y: 4, z: 8, core: 2. Of those that a mesh axis runs over, the one named last changes fastest.
Arguments:
- spectral: bfloat16 [4, 128, 2, 640, 640], P('fld', None, None, 'wave'), may hold values from -0.4375 to 0.4375
- legendre: bfloat16 [640, 640, 256], P('wave', None, 'fld'), may hold values from -0.25 to 0.25
- wave_of_row: int32 [640], replicated, may hold values from 0 to 639, each once
- row_points: int32 [256], replicated, may hold values from 20 to 5132, as said below
- lat_slot: int32 [256], replicated, may hold values from 0 to 255, each once
- field_slot: int32 [128], replicated, may hold values from 0 to 127, each once
Outputs:
- grid: bfloat16 [4, 128, 256, 5136], P('fld', 'wave')
Inputs may be any that keep to these rules, and one draw needn't show every extreme that they name: `wave_of_row`: each wavenumber 0 to 639 is held by exactly one row. `row_points`: window latitude j is a distinct row i of the octahedral grid's northern half, with 4 i + 16 points; the window's rows come in pairs i and (5120) / 4 - i, so that the points of each pair sum to 5152; the pair with i = 1 is always in the window. `lat_slot`: each window latitude fills exactly one slot. `field_slot`: each level-field pair of a group fills exactly one writer slot.
All inputs are finite; a program needn't handle non-finite values.
Results may differ from a plain program's by a relative error of at most 0.0055.
Values may be sent and summed in bfloat16 or wider, within the bound.
A program may use at most 128 MiB of HBM per device.

v0:
```python
import math

import jax
import jax.numpy as jnp
from jax import lax
from jax.sharding import PartitionSpec as P

LON = 5136


def twiddle(wave_numbers, points):
    step_count = 64
    outer_count = (LON + step_count - 1) // step_count
    outer = jnp.arange(outer_count, dtype=jnp.int32) * step_count
    inner = jnp.arange(step_count, dtype=jnp.int32)
    scale = 2.0 * math.pi / points.astype(jnp.float32)
    outer_phase = (wave_numbers[:, None] * outer[None, :] % points).astype(jnp.float32) * scale
    inner_phase = (wave_numbers[:, None] * inner[None, :] % points).astype(jnp.float32) * scale
    outer_cos = jnp.cos(outer_phase)[:, :, None]
    outer_sin = jnp.sin(outer_phase)[:, :, None]
    inner_cos = jnp.cos(inner_phase)[:, None, :]
    inner_sin = jnp.sin(inner_phase)[:, None, :]
    rows = wave_numbers.shape[0]
    cos_full = (outer_cos * inner_cos - outer_sin * inner_sin).reshape(
        rows, outer_count * step_count
    )[:, :LON]
    sin_full = (outer_sin * inner_cos + outer_cos * inner_sin).reshape(
        rows, outer_count * step_count
    )[:, :LON]
    longitudes = jnp.arange(LON, dtype=jnp.int32)
    weight = jnp.where(wave_numbers == 0, 1.0, 2.0).astype(jnp.float32)[:, None]
    alive_mask = (2 * wave_numbers[:, None] < points) & (longitudes[None, :] < points)
    cosine = jnp.where(alive_mask, weight * cos_full, 0.0)
    sine_part = jnp.where(alive_mask, -weight * sin_full, 0.0)
    return jnp.stack([cosine, sine_part]).astype(jnp.bfloat16)


def longitude(coeff_rows, wave_numbers, slot_points):
    by_latitude = jnp.moveaxis(coeff_rows, 1, 0)

    def one_latitude(inputs):
        coeff_block, points = inputs
        phase_table = twiddle(wave_numbers, points)
        result = jnp.einsum(
            "rcp,crk->pk", coeff_block, phase_table, preferred_element_type=jnp.float32
        )
        return result.astype(jnp.bfloat16)

    grid_rows = lax.map(one_latitude, (by_latitude, slot_points))
    return jnp.moveaxis(grid_rows, 0, 1)


def local(spectral, legendre, wave_of_row, row_points, lat_slot, field_slot):
    rows_here = legendre.shape[0]
    degree_count = legendre.shape[1]
    lat_count = lat_slot.shape[0]
    my_waves = lax.dynamic_slice_in_dim(wave_of_row, lax.axis_index("wave") * rows_here, rows_here)
    degrees = jnp.arange(degree_count, dtype=jnp.int32)
    alive_mask = degrees[None, :] >= my_waves[:, None]
    masked = jnp.where(alive_mask[None, None], spectral[0], jnp.zeros((), jnp.bfloat16))
    result = jnp.einsum(
        "pcrn,rnj->rjcp",
        masked,
        lax.all_gather(legendre, "fld", axis=2, tiled=True),
        preferred_element_type=jnp.float32,
    )
    fourier_all = result.astype(jnp.bfloat16)
    fourier = jnp.take(jnp.take(fourier_all, lat_slot, axis=1), field_slot, axis=3)
    slot_points = jnp.take(row_points, lat_slot)
    slots_here = lat_count // lax.axis_size("wave")
    my_points = lax.dynamic_slice_in_dim(
        slot_points, lax.axis_index("wave") * slots_here, slots_here
    )
    built = longitude(
        lax.all_to_all(fourier, "wave", split_axis=1, concat_axis=0, tiled=True),
        wave_of_row,
        my_points,
    )
    grid_rows = lax.all_to_all(built, "wave", split_axis=0, concat_axis=1, tiled=True)
    return grid_rows[None]


def solution(mesh):
    in_specs = (P("fld", None, None, "wave", None), P("wave", None, "fld"), P(), P(), P(), P())
    out_specs = P("fld", "wave", None, None)
    return jax.shard_map(local, mesh=mesh, in_specs=in_specs, out_specs=out_specs, check_vma=False)
```

profile of v0, /device:TPU:1, one launch (start us, length us, event | category | flops | bytes accessed | tf_op | source)
XLA Modules:
  0.0 443.9 jit_solution(10256979436770118333)
XLA Ops:
  12.8 4.7 %broadcast_select_fusion = bf16[128,2,10,640]{3,1,2,0:T(2,128)(2,1)S(1)} fusion(pred[10,640]{1,0:T(8,128)(4,1)S(1)} %iota_compare_fusion.1, bf16[1,128,2,10,640]{4,2,3,1,0:T(2,128)(2,1)} %param.8), kind=kLoop, calls=%fused_computation.49 | loop fusion | flops 1638400 | bytes 6560000 | tf_op jit(solution)/shard_map/jit(_where)/select_n | solution.py:60
  17.5 38.7 %all-gather.2.cloned.1.call-done = bf16[10,640,256]{1,2,0:T(8,128)(2,1)} async-done(((bf16[10,640,64]{1,2,0:T(8,128)(2,1)}), bf16[10,640,256]{1,2,0:T(8,128)(2,1)}) %all-gather.2.cloned.1.call-update) | async-done | bytes 3276816 | tf_op jit(solution)/shard_map/all_gather | solution.py:64
  56.2 4.2 fusion.46
  63.8 4.4 gather_fusion
  78.1 4.3 copy.32
  82.4 10.8 %all-to-all-start = ((bf16[10,256,2,128]{3,2,0,1:T(2,128)(2,1)}), bf16[10,256,2,128]{3,2,0,1:T(2,128)(2,1)S(1)}, u32[]{:S(2)}, u32[]{:S(2)}) async-start(bf16[10,256,2,128]{3,2,0,1:T(2,128)(2,1)} %copy.32), calls=%async_computation | async-start | bytes 2621440 | tf_op jit(solution)/shard_map/all_to_all | solution.py:75
  93.4 34.1 %all-to-all-done = bf16[10,256,2,128]{3,2,0,1:T(2,128)(2,1)S(1)} async-done(((bf16[10,256,2,128]{3,2,0,1:T(2,128)(2,1)}), bf16[10,256,2,128]{3,2,0,1:T(2,128)(2,1)S(1)}, u32[]{:S(2)}, u32[]{:S(2)}) %all-to-all-start) | async-done | bytes 1310752 | tf_op jit(solution)/shard_map/all_to_all | solution.py:75
  129.8 149.0 %while.10 = (s32[]{:T(128)}, bf16[4,128,5136]{1,2,0:T(8,128)(2,1)}, bf16[4,640,2,128]{3,2,0,1:T(2,128)(2,1)S(1)}, s32[640]{0:T(1024)S(1)}, s32[4]{0:T(128)S(1)}, /*index=5*/s32[]{:T(128)}, f32[]{:T(128)}, s32[]{:T(128)}) while((s32[]{:T(128)}, bf16[4,128,5136]{1,2,0:T(8,128)(2,1)}, bf16[4,640,2,128]{3,2,0,1:T(2,128)(2,1)S(1)}, ...), condition=%wide.region_1.2_spmd, body=%wide.region_0.1_spmd.sunk | while | flops 1734048256 | bytes 82950744 | solution.py:49
  138.1 12.6 %multiply_subtract_fusion.2 = (f32[640,81,64]{0,2,1:T(8,128)}, f32[640,81,64]{0,2,1:T(8,128)}) fusion(f32[640,64]{0,1:T(8,128)S(1)} %get-tuple-element.111, f32[640,81]{0,1:T(8,128)S(1)} %get-tuple-element.112, f32[640,64]{0,1:T(8,128)S(1)} %get-tuple-element.113, f32[640,81]{0,1:T(8,128)S(1)} %get-tuple-element.114), kind=kLoop, calls=%fused_computation.6.clone.1 | loop fusion | flops 19906560 | bytes 27284480 | tf_op jit(solution)/shard_map/while/body/eval_jaxpr/sub | solution.py:24
  152.1 10.1 %fusion.61 = (bf16[1,640,5136]{1,2,0:T(8,128)(2,1)S(1)}, bf16[1,640,5136]{1,2,0:T(8,128)(2,1)S(1)}) fusion(f32[640,5184]{0,1:T(8,128)} %bitcast.64, f32[640]{0:T(1024)S(1)} %get-tuple-element.116, pred[640]{0:T(1024)(128)(4,1)S(1)} %multiply_compare_fusion.2, pred[5136]{0:T(1024)(128)(4,1)S(1)} %iota_compare_fusion.3, f32[640,5184]{0,1:T(8,128)} %bitcast.65, ...), kind=kLoop, calls=%fused_computation.20.clone.1 | loop fusion | flops 23009280 | bytes 39455376 | tf_op jit(solution)/shard_map/while/body/eval_jaxpr/stack | solution.py:35
  162.4 4.8 %fusion.62 = bf16[4,128,5136]{1,2,0:T(8,128)(2,1)} fusion(bf16[4,128,5136]{1,2,0:T(8,128)(2,1)} %get-tuple-element.130, s32[]{:T(128)} %get-tuple-element.129, bf16[1,640,5136]{1,2,0:T(8,128)(2,1)S(1)} %get-tuple-element.119, bf16[1,640,5136]{1,2,0:T(8,128)(2,1)S(1)} %get-tuple-element.120, bf16[1,640,2,128]{3,2,0,1:T(2,128)(2,1)S(1)} %constant_dynamic-slice_fusion.2), kind=kOutput, calls=%fused_computation.18.clone.1 | convolution fusion | flops 1690195968 | bytes 14791168 | tf_op jit(solution)/shard_map/while/body/eval_jaxpr/rcp,crk->pk/dot_general | solution.py:44
  175.3 12.6 %multiply_subtract_fusion.2 = (f32[640,81,64]{0,2,1:T(8,128)}, f32[640,81,64]{0,2,1:T(8,128)}) fusion(f32[640,64]{0,1:T(8,128)S(1)} %get-tuple-element.111, f32[640,81]{0,1:T(8,128)S(1)} %get-tuple-element.112, f32[640,64]{0,1:T(8,128)S(1)} %get-tuple-element.113, f32[640,81]{0,1:T(8,128)S(1)} %get-tuple-element.114), kind=kLoop, calls=%fused_computation.6.clone.1 | loop fusion | flops 19906560 | bytes 27284480 | tf_op jit(solution)/shard_map/while/body/eval_jaxpr/sub | solution.py:24
  189.2 10.1 %fusion.61 = (bf16[1,640,5136]{1,2,0:T(8,128)(2,1)S(1)}, bf16[1,640,5136]{1,2,0:T(8,128)(2,1)S(1)}) fusion(f32[640,5184]{0,1:T(8,128)} %bitcast.64, f32[640]{0:T(1024)S(1)} %get-tuple-element.116, pred[640]{0:T(1024)(128)(4,1)S(1)} %multiply_compare_fusion.2, pred[5136]{0:T(1024)(128)(4,1)S(1)} %iota_compare_fusion.3, f32[640,5184]{0,1:T(8,128)} %bitcast.65, ...), kind=kLoop, calls=%fused_computation.20.clone.1 | loop fusion | flops 23009280 | bytes 39455376 | tf_op jit(solution)/shard_map/while/body/eval_jaxpr/stack | solution.py:35
  199.6 4.8 %fusion.62 = bf16[4,128,5136]{1,2,0:T(8,128)(2,1)} fusion(bf16[4,128,5136]{1,2,0:T(8,128)(2,1)} %get-tuple-element.130, s32[]{:T(128)} %get-tuple-element.129, bf16[1,640,5136]{1,2,0:T(8,128)(2,1)S(1)} %get-tuple-element.119, bf16[1,640,5136]{1,2,0:T(8,128)(2,1)S(1)} %get-tuple-element.120, bf16[1,640,2,128]{3,2,0,1:T(2,128)(2,1)S(1)} %constant_dynamic-slice_fusion.2), kind=kOutput, calls=%fused_computation.18.clone.1 | convolution fusion | flops 1690195968 | bytes 14791168 | tf_op jit(solution)/shard_map/while/body/eval_jaxpr/rcp,crk->pk/dot_general | solution.py:44
  212.4 12.6 %multiply_subtract_fusion.2 = (f32[640,81,64]{0,2,1:T(8,128)}, f32[640,81,64]{0,2,1:T(8,128)}) fusion(f32[640,64]{0,1:T(8,128)S(1)} %get-tuple-element.111, f32[640,81]{0,1:T(8,128)S(1)} %get-tuple-element.112, f32[640,64]{0,1:T(8,128)S(1)} %get-tuple-element.113, f32[640,81]{0,1:T(8,128)S(1)} %get-tuple-element.114), kind=kLoop, calls=%fused_computation.6.clone.1 | loop fusion | flops 19906560 | bytes 27284480 | tf_op jit(solution)/shard_map/while/body/eval_jaxpr/sub | solution.py:24
  226.4 10.1 %fusion.61 = (bf16[1,640,5136]{1,2,0:T(8,128)(2,1)S(1)}, bf16[1,640,5136]{1,2,0:T(8,128)(2,1)S(1)}) fusion(f32[640,5184]{0,1:T(8,128)} %bitcast.64, f32[640]{0:T(1024)S(1)} %get-tuple-element.116, pred[640]{0:T(1024)(128)(4,1)S(1)} %multiply_compare_fusion.2, pred[5136]{0:T(1024)(128)(4,1)S(1)} %iota_compare_fusion.3, f32[640,5184]{0,1:T(8,128)} %bitcast.65, ...), kind=kLoop, calls=%fused_computation.20.clone.1 | loop fusion | flops 23009280 | bytes 39455376 | tf_op jit(solution)/shard_map/while/body/eval_jaxpr/stack | solution.py:35
  236.7 4.8 %fusion.62 = bf16[4,128,5136]{1,2,0:T(8,128)(2,1)} fusion(bf16[4,128,5136]{1,2,0:T(8,128)(2,1)} %get-tuple-element.130, s32[]{:T(128)} %get-tuple-element.129, bf16[1,640,5136]{1,2,0:T(8,128)(2,1)S(1)} %get-tuple-element.119, bf16[1,640,5136]{1,2,0:T(8,128)(2,1)S(1)} %get-tuple-element.120, bf16[1,640,2,128]{3,2,0,1:T(2,128)(2,1)S(1)} %constant_dynamic-slice_fusion.2), kind=kOutput, calls=%fused_computation.18.clone.1 | convolution fusion | flops 1690195968 | bytes 14791168 | tf_op jit(solution)/shard_map/while/body/eval_jaxpr/rcp,crk->pk/dot_general | solution.py:44
  249.6 12.6 %multiply_subtract_fusion.2 = (f32[640,81,64]{0,2,1:T(8,128)}, f32[640,81,64]{0,2,1:T(8,128)}) fusion(f32[640,64]{0,1:T(8,128)S(1)} %get-tuple-element.111, f32[640,81]{0,1:T(8,128)S(1)} %get-tuple-element.112, f32[640,64]{0,1:T(8,128)S(1)} %get-tuple-element.113, f32[640,81]{0,1:T(8,128)S(1)} %get-tuple-element.114), kind=kLoop, calls=%fused_computation.6.clone.1 | loop fusion | flops 19906560 | bytes 27284480 | tf_op jit(solution)/shard_map/while/body/eval_jaxpr/sub | solution.py:24
  263.6 10.1 %fusion.61 = (bf16[1,640,5136]{1,2,0:T(8,128)(2,1)S(1)}, bf16[1,640,5136]{1,2,0:T(8,128)(2,1)S(1)}) fusion(f32[640,5184]{0,1:T(8,128)} %bitcast.64, f32[640]{0:T(1024)S(1)} %get-tuple-element.116, pred[640]{0:T(1024)(128)(4,1)S(1)} %multiply_compare_fusion.2, pred[5136]{0:T(1024)(128)(4,1)S(1)} %iota_compare_fusion.3, f32[640,5184]{0,1:T(8,128)} %bitcast.65, ...), kind=kLoop, calls=%fused_computation.20.clone.1 | loop fusion | flops 23009280 | bytes 39455376 | tf_op jit(solution)/shard_map/while/body/eval_jaxpr/stack | solution.py:35
  273.9 4.8 %fusion.62 = bf16[4,128,5136]{1,2,0:T(8,128)(2,1)} fusion(bf16[4,128,5136]{1,2,0:T(8,128)(2,1)} %get-tuple-element.130, s32[]{:T(128)} %get-tuple-element.129, bf16[1,640,5136]{1,2,0:T(8,128)(2,1)S(1)} %get-tuple-element.119, bf16[1,640,5136]{1,2,0:T(8,128)(2,1)S(1)} %get-tuple-element.120, bf16[1,640,2,128]{3,2,0,1:T(2,128)(2,1)S(1)} %constant_dynamic-slice_fusion.2), kind=kOutput, calls=%fused_computation.18.clone.1 | convolution fusion | flops 1690195968 | bytes 14791168 | tf_op jit(solution)/shard_map/while/body/eval_jaxpr/rcp,crk->pk/dot_general | solution.py:44
  278.8 10.0 %copy.36 = bf16[4,128,5136]{2,0,1:T(4,128)(2,1)} copy(bf16[4,128,5136]{1,2,0:T(8,128)(2,1)} %get-tuple-element.32) | data formatting | bytes 10518528 | tf_op jit(solution)/shard_map/while | solution.py:49
  288.8 127.4 %all_to_all.33 = bf16[128,4,5136]{2,1,0:T(4,128)(2,1)S(1)} all-to-all(bf16[128,4,5136]{2,1,0:T(4,128)(2,1)} %bitcast.66), channel_id=1, replica_groups=mesh['wave'=64,'fld'=4] {'wave'}, dimensions={0} | all-to-all | bytes 10518528 | tf_op jit(solution)/shard_map/all_to_all | solution.py:79
  416.2 6.8 %copy.37 = bf16[2,64,4,5136]{3,0,2,1:T(2,128)(2,1)} copy(bf16[2,64,4,5136]{3,2,0,1:T(4,128)(2,1)S(1)} %bitcast.67) | data formatting | bytes 10518528 | tf_op jit(solution)/shard_map/all_to_all | solution.py:79
  423.0 14.0 %copy.38 = bf16[1,2,256,5136]{2,3,1,0:T(8,128)(2,1)} copy(bf16[1,2,256,5136]{3,1,2,0:T(2,128)(2,1)} %bitcast.68) | data formatting | bytes 10518528 | tf_op jit(solution)/shard_map/broadcast_in_dim | solution.py:80
  (58 shorter events, 52.1 us)
Async XLA Ops:
  6.5 2.2 copy-start
  6.5 49.6 %all-gather.2.cloned.1.call-start = ((), (), s32[]{:S(2)}) async-start(), calls=%async_computation.2 | async-start | bytes 4096000 | tf_op jit(solution)/shard_map/all_gather | solution.py:64
  82.4 47.3 %copy-start.2 = (s32[640]{0:T(1024)S(1)}, s32[640]{0:T(1024)}, u32[]{:S(2)}) copy-start(s32[640]{0:T(1024)} %param.10) | copy-start | bytes 7684
  82.4 45.0 %all-to-all-start = ((bf16[10,256,2,128]{3,2,0,1:T(2,128)(2,1)}), bf16[10,256,2,128]{3,2,0,1:T(2,128)(2,1)S(1)}, u32[]{:S(2)}, u32[]{:S(2)}) async-start(bf16[10,256,2,128]{3,2,0,1:T(2,128)(2,1)} %copy.32), calls=%async_computation | async-start | bytes 2621440 | tf_op jit(solution)/shard_map/all_to_all | solution.py:75
  423.0 14.1 %copy-start.1 = (s32[256]{0:T(256)S(1)}, s32[256]{0:T(256)}, u32[]{:S(2)}) copy-start(s32[256]{0:T(256)} %param.11) | copy-start | bytes 3076
Sparse Core Ops, SparseCore 0:
  9.2 46.9 all-gather.1
where the time goes:
time: 445 us; the launch traced here: 444 us
  other arithmetic  127 us (29%)
  blocking collectives  127 us (29%)
  waiting for transfers between devices  73.5 us (17%)
  local copies, waits for them, and re-layouts  58.9 us (13%)
  matrix products  23.5 us (5%)
  between operations  13.5 us (3%)
  starting transfers between devices  10.8 us (2%)
  loops' own time  8.92 us (2%)
    all_to_all x1, blocking collectives, local(): lax.all_to_all(built, 'wave', split_axis=0, concat_axis=1, tiled=True)  127 us
    sub x4, other arithmetic, twiddle(): outer_cos * inner_cos - outer_sin * inner_sin  50.3 us
    another operation x4, other arithmetic, twiddle(): return jnp.stack([cosine, sine_part]).astype(jnp.bfloat16)  40.2 us
    all_gather x1, waiting for transfers between devices, local(): lax.all_gather(legendre, 'fld', axis=2, tiled=True)  38.7 us
    all_to_all x1, waiting for transfers between devices, local(): lax.all_to_all(fourier, 'wave', split_axis=1, concat_axis=0, tiled=True)  34.1 us
    dot_general x4, matrix products, one_latitude(): jnp.einsum('rcp,crk->pk', coeff_block, phase_table, preferred_element_typ...  19.3 us
    broadcast_in_dim x1, local copies, waits for them, and re-layouts, local(): return grid_rows[None]  14 us
    cos x4, other arithmetic, twiddle(): outer_cos = jnp.cos(outer_phase)[:, :, None]  12.3 us
  transfers between devices with their start and end apart: 2, of which 2 were waited for; matrix products, arithmetic and copies ran while one was open for 2% of the time, Pallas kernels for 0%

commit v1 on v0

v1 whole, which is shorter than its diff:
```python
import functools
import math

import jax
import jax.numpy as jnp
from jax import lax
from jax.experimental import pallas as pl
from jax.experimental.pallas import tpu as pltpu
from jax.sharding import PartitionSpec as P

LANES = 128
SUBLANES = 8
COARSE = 48


def turn(product, points, inverse):
    residue = product - jnp.round(product * inverse) * points
    x = residue * inverse * (math.pi / 2)
    y = x * x
    s = x * (1.0 + y * (-1.0 / 6 + y * (1.0 / 120 + y * (-1.0 / 5040))))
    c = 1.0 + y * (-0.5 + y * (1.0 / 24 + y * (-1.0 / 720 + y * (1.0 / 40320))))
    for _ in range(2):
        c, s = 1.0 - 2.0 * s * s, 2.0 * s * c
    return c, s


def times(a, b):
    return a[0] * b[0] - a[1] * b[1], a[0] * b[1] + a[1] * b[0]


def powers(base, count):
    one = (jnp.ones_like(base[0]), jnp.zeros_like(base[0]))
    out = [one, base]
    for i in range(2, count):
        out.append(times(out[i // 2], out[i - i // 2]))
    return out[:count]


def dot_nt(a, b):
    return lax.dot_general(a, b, (((1,), (1,)), ((), ())), preferred_element_type=jnp.float32)


def zonal_kernel(
    four_ref, wave_ref, points_ref, slot_ref, out_ref,
    live, npts, inner_c, inner_s, step_c, step_s, outer_c, outer_s, lead_r, lead_i, left, table, rows,
):
    lat = slot_ref.shape[1]
    waves = wave_ref.shape[1]
    tiles = waves // LANES
    lon = out_ref.shape[1]
    blocks = pl.cdiv(lon, LANES)
    bf16, f32 = jnp.bfloat16, jnp.float32

    held = lax.broadcasted_iota(jnp.int32, (lat, lat), 0)
    by_lane = jnp.where(held == slot_ref[...], 1.0, 0.0).astype(bf16)
    eye = jnp.where(held == lax.broadcasted_iota(jnp.int32, (lat, lat), 1), 1.0, 0.0).astype(bf16)
    chosen = dot_nt(eye, by_lane)
    npts[...] = jnp.broadcast_to(
        jnp.sum(chosen * points_ref[...].astype(f32), axis=1, keepdims=True), (lat, LANES)
    )
    chosen = chosen.astype(bf16)
    for part in range(4):
        moved = dot_nt(chosen, four_ref[part])
        for t in range(tiles):
            live[part, t] = moved[:, t * LANES:(t + 1) * LANES]

    def block(i, carry):
        s0 = pl.multiple_of(i * SUBLANES, SUBLANES)
        points = npts[pl.ds(s0, SUBLANES), :]
        inverse = 1.0 / points
        for t in range(tiles):
            m = jnp.broadcast_to(wave_ref[:, t * LANES:(t + 1) * LANES].astype(f32), points.shape)
            weight = jnp.where(2.0 * m < points, jnp.where(m == 0.0, 1.0, 2.0), 0.0)
            for j, (c, s) in enumerate(powers(turn(m, points, inverse), 8)):
                inner_c[t, pl.ds(j * 8, 8), :] = c
                inner_s[t, pl.ds(j * 8, 8), :] = s
            steps = powers(turn(m * 8.0, points, inverse), 9)
            for j, (c, s) in enumerate(steps):
                step_c[t, pl.ds(j * 8, 8), :] = c
                step_s[t, pl.ds(j * 8, 8), :] = s
            for j, (c, s) in enumerate(powers(turn(m * 128.0, points, inverse), 8)):
                outer_c[t, pl.ds(j * 8, 8), :] = c
                outer_s[t, pl.ds(j * 8, 8), :] = s
            far = powers(turn(m * 1024.0, points, inverse), COARSE // 8)
            for p in range(2):
                value = (
                    live[2 * p, t, pl.ds(s0, SUBLANES), :] * weight,
                    live[2 * p + 1, t, pl.ds(s0, SUBLANES), :] * weight,
                )
                value = times(value, steps[8])
                for a, w in enumerate(far):
                    r, im = times(value, w) if a else value
                    row = (p * (COARSE // 8) + a) * 8
                    lead_r[t, pl.ds(row, 8), :] = r
                    lead_i[t, pl.ds(row, 8), :] = im

        def one(l, buf):
            def bcast(ref, t, row):
                return ref[t, pl.ds(row * 8 + l, 8, stride=0), :]

            def spread(ref, t):
                return ref[t, pl.ds(l, 8, stride=8), :]

            for t in range(tiles):
                ic, isn = spread(inner_c, t), spread(inner_s, t)
                cs, ss = [None] * 16, [None] * 16
                cs[8], ss[8] = ic, isn
                for j in range(1, 9):
                    wc, ws = bcast(step_c, t, j), bcast(step_s, t, j)
                    a, b, c, d = ic * wc, isn * ws, isn * wc, ic * ws
                    if j < 8:
                        cs[8 + j], ss[8 + j] = a - b, c + d
                    cs[8 - j], ss[8 - j] = a + b, c - d
                here = pl.ds(t * LANES, LANES)
                there = pl.ds(waves + t * LANES, LANES)
                for q in range(8):
                    table[buf, pl.ds(q * 16, 16), here] = jnp.concatenate(
                        [cs[2 * q], cs[2 * q + 1]], axis=0).astype(bf16)
                    table[buf, pl.ds(q * 16, 16), there] = jnp.concatenate(
                        [ss[2 * q], ss[2 * q + 1]], axis=0).astype(bf16)
                oc, os = spread(outer_c, t), spread(outer_s, t)
                for q in range(COARSE // 8):
                    res, ims = [], []
                    for h in range(2):
                        fr, fi = bcast(lead_r, t, 2 * q + h), bcast(lead_i, t, 2 * q + h)
                        res.append(fr * oc - fi * os)
                        ims.append(-(fr * os) - fi * oc)
                    left[buf, pl.ds(q * 16, 16), here] = jnp.concatenate(res, axis=0).astype(bf16)
                    left[buf, pl.ds(q * 16, 16), there] = jnp.concatenate(ims, axis=0).astype(bf16)
            rows[pl.ds(s0 + l, 2 * COARSE, stride=lat), :] = dot_nt(left[buf], table[buf])

        def pair(h, carry):
            one(2 * h, 0)
            one(2 * h + 1, 1)
            return carry

        return lax.fori_loop(0, SUBLANES // 2, pair, carry)

    lax.fori_loop(0, lat // SUBLANES, block, 0)

    small = eye[:LANES, :LANES]
    lane = lax.broadcasted_iota(jnp.int32, (lat, LANES), 1).astype(f32)

    def turned(p, a):
        start = pl.multiple_of((p * COARSE + a) * lat, lat)
        value = rows[pl.ds(start, lat), :]
        first = jnp.float32(a * LANES) if isinstance(a, int) else (a * LANES).astype(f32)
        value = jnp.where(lane + first < npts[...], value, 0.0).astype(bf16)
        return dot_nt(small, value).astype(bf16)

    for p in range(2):
        def whole(a, carry, p=p):
            out_ref[p, pl.ds(pl.multiple_of(a * LANES, LANES), LANES), :] = turned(p, a)
            return carry

        lax.fori_loop(0, blocks - 1, whole, 0)
        last = (blocks - 1) * LANES
        out_ref[p, last:, :] = turned(p, blocks - 1)[:lon - last]


def zonal(four, wave_of_row, row_points, lat_slot, lon):
    _, waves, lat = four.shape
    tiles = waves // LANES
    f32 = jnp.float32
    vmem = pl.BlockSpec(memory_space=pltpu.VMEM)

    def scratch(count):
        return pltpu.VMEM((tiles, count * 8, LANES), f32)

    return pl.pallas_call(
        zonal_kernel,
        out_shape=jax.ShapeDtypeStruct((2, lon, lat), jnp.bfloat16),
        in_specs=[vmem] * 4,
        out_specs=vmem,
        scratch_shapes=[
            pltpu.VMEM((4, tiles, lat, LANES), f32),
            pltpu.VMEM((lat, LANES), f32),
            scratch(8), scratch(8), scratch(9), scratch(9), scratch(8), scratch(8),
            scratch(2 * COARSE // 8), scratch(2 * COARSE // 8),
            pltpu.VMEM((2, 2 * COARSE, 2 * waves), jnp.bfloat16),
            pltpu.VMEM((2, LANES, 2 * waves), jnp.bfloat16),
            pltpu.VMEM((2 * COARSE * lat, LANES), f32),
        ],
        compiler_params=pltpu.CompilerParams(vmem_limit_bytes=48 * 1024 * 1024),
        cost_estimate=pl.CostEstimate(
            flops=2 * lat * 2 * COARSE * LANES * 2 * waves, bytes_accessed=7 << 20, transcendentals=0
        ),
    )(four, wave_of_row[None], row_points[None], lat_slot[None])


LON = 5136


def local(spectral, legendre, wave_of_row, row_points, lat_slot, field_slot):
    rows_here, degree_count, _ = legendre.shape
    my_waves = lax.dynamic_slice_in_dim(wave_of_row, lax.axis_index("wave") * rows_here, rows_here)
    degrees = jnp.arange(degree_count, dtype=jnp.int32)
    alive_mask = degrees[None, :] >= my_waves[:, None]
    masked = jnp.where(alive_mask[None, None], spectral[0], jnp.zeros((), jnp.bfloat16))
    fourier = jnp.einsum(
        "pcrn,rnj->pcrj",
        masked,
        lax.all_gather(legendre, "fld", axis=2, tiled=True),
        preferred_element_type=jnp.float32,
    ).astype(jnp.bfloat16)
    fourier = jnp.take(fourier, field_slot, axis=0)
    fourier = lax.all_to_all(fourier, "wave", split_axis=0, concat_axis=2, tiled=True)
    fourier = fourier.reshape(4, -1, lat_slot.shape[0])
    grid = zonal(fourier, wave_of_row, row_points, lat_slot, LON)
    return jnp.transpose(grid, (0, 2, 1))[None]


def solution(mesh):
    in_specs = (P("fld", None, None, "wave", None), P("wave", None, "fld"), P(), P(), P(), P())
    out_specs = P("fld", "wave", None, None)
    return jax.shard_map(local, mesh=mesh, in_specs=in_specs, out_specs=out_specs, check_vma=False)
```

time: 445 us -> 228 us (0.51)
  blocking collectives: 127 us -> 0 us
  other arithmetic: 127 us -> 8.51 us
  Pallas kernels: 0 us -> 106 us
  local copies, waits for them, and re-layouts: 58.9 us -> 9.26 us
  matrix products: 23.5 us -> 3.15 us
  loops' own time: 8.92 us -> 0 us
    all_to_all x1 -> x0, blocking collectives: 127 us -> none  [local(): lax.all_to_all(built, 'wave', split_axis=0, concat_axis=1, tiled=True)]
    pallas_call x0 -> x1, Pallas kernels: none -> 106 us  [zonal(): pl.pallas_call(zonal_kernel, out_shape=jax.ShapeDtypeStruct((2, lon, lat)...]
    sub x4 -> x0, other arithmetic: 50.3 us -> none  [twiddle(): outer_cos * inner_cos - outer_sin * inner_sin]
    another operation x4 -> x0, other arithmetic: 40.2 us -> none  [twiddle(): return jnp.stack([cosine, sine_part]).astype(jnp.bfloat16)]
    cos x8 -> x0, other arithmetic: 21.1 us -> none  [the longest x4 12.3 us: twiddle(): outer_cos = jnp.cos(outer_phase)[:, :, None]]
    dot_general x5 -> x1, matrix products: 23.5 us -> 3.15 us  [local(): jnp.einsum('pcrn,rnj->pcrj', masked, lax.all_gather(legendre, 'fld', axis...]
    broadcast_in_dim x1, local copies, waits for them, and re-layouts: 14 us -> 0.01 us  [zonal(): wave_of_row[None]]
    while x1 -> x0, local copies, waits for them, and re-layouts: 10 us -> none  [longitude(): grid_rows = lax.map(one_latitude, (by_latitude, slot_points))]
  transfers between devices with their start and end apart: 2 -> 2, of which waited for: 2 -> 2; matrix products, arithmetic and copies ran while one was open for 2% -> 3% of each run, Pallas kernels for 0% -> 0%
where the time goes in v1:
time: 228 us
  Pallas kernels  106 us (46%)
  waiting for transfers between devices  76.9 us (34%)
  between operations  13.5 us (6%)
  starting transfers between devices  10.7 us (5%)
  local copies, waits for them, and re-layouts  9.26 us (4%)
  other arithmetic  8.51 us (4%)
  matrix products  3.15 us (1%)
    pallas_call x1, Pallas kernels, zonal(): pl.pallas_call(zonal_kernel, out_shape=jax.ShapeDtypeStruct((2, lon, lat)...  106 us
    all_gather x1, waiting for transfers between devices, local(): lax.all_gather(legendre, 'fld', axis=2, tiled=True)  42 us
    all_to_all x1, waiting for transfers between devices, local(): lax.all_to_all(fourier, 'wave', split_axis=0, concat_axis=2, tiled=True)  34.1 us
    all_to_all x1, starting transfers between devices, local(): lax.all_to_all(fourier, 'wave', split_axis=0, concat_axis=2, tiled=True)  10.7 us
    select_n x1, other arithmetic, local(): jnp.where(alive_mask[None, None], spectral[0], jnp.zeros((), jnp.bfloat16))  4.72 us
  transfers between devices with their start and end apart: 2, of which 2 were waited for; matrix products, arithmetic and copies ran while one was open for 3% of the time, Pallas kernels for 0%

profile of v1, /device:TPU:1, one launch (start us, length us, event | category | flops | bytes accessed | tf_op | source)
XLA Modules:
  0.0 227.7 jit_solution(9848853841973535476)
XLA Ops:
  6.5 0.0 all-gather.2.cloned.1.call-start
  6.5 0.7 all-gather.2.cloned.1.call-update
  7.3 0.8 dynamic_slice.3
  8.0 0.7 compare_select_fusion
  8.7 0.7 compare_and_fusion
  9.4 0.1 iota_compare_fusion
  9.4 4.7 %broadcast_select_fusion = bf16[128,2,10,640]{3,1,2,0:T(2,128)(2,1)S(1)} fusion(pred[10,640]{1,0:T(8,128)(4,1)S(1)} %iota_compare_fusion, bf16[1,128,2,10,640]{4,2,3,1,0:T(2,128)(2,1)} %param.6), kind=kLoop, calls=%fused_computation.1 | loop fusion | flops 1638400 | bytes 6560000 | tf_op jit(solution)/shard_map/jit(_where)/select_n | solution.py:199
  14.2 42.0 %all-gather.2.cloned.1.call-done = bf16[10,640,256]{1,2,0:T(8,128)(2,1)} async-done(((bf16[10,640,64]{1,2,0:T(8,128)(2,1)}), bf16[10,640,256]{1,2,0:T(8,128)(2,1)}) %all-gather.2.cloned.1.call-update) | async-done | bytes 3276816 | tf_op jit(solution)/shard_map/all_gather | solution.py:203
  56.2 3.1 %fusion.8 = bf16[128,2,10,256]{3,0,1,2:T(8,128)(2,1)S(1)} fusion(bf16[10,640,256]{1,2,0:T(8,128)(2,1)} %all-gather.2.cloned.1.call-done, bf16[128,2,10,640]{3,1,2,0:T(2,128)(2,1)S(1)} %broadcast_select_fusion), kind=kOutput, calls=%fused_computation.7 | convolution fusion | flops 839516160 | bytes 7864320 | tf_op jit(solution)/shard_map/pcrn,rnj->pcrj/dot_general | solution.py:200
  59.3 1.3 copy.10
  60.7 3.2 %gather_fusion = bf16[128,2,10,256]{3,1,2,0:T(2,128)(2,1)S(1)} fusion(bf16[128,2,10,256]{3,1,2,0:T(2,128)(2,1)S(1)} %copy.10, s32[1024]{0:T(1024)S(1)} %pad_clamp_fusion), kind=kCustom, calls=%fused_computation | custom fusion | bytes 2621952 | tf_op jit(solution)/shard_map/jit(_take)/gather | solution.py:206
  63.9 0.0 copy-start.2
  63.9 2.4 %broadcast_select_fusion.1 = bf16[128,2,10,256]{3,1,2,0:T(2,128)(2,1)} fusion(bf16[128,2,10,256]{3,1,2,0:T(2,128)(2,1)S(1)} %gather_fusion, pred[128]{0:T(512)(128)(4,1)S(1)} %compare_and_fusion), kind=kLoop, calls=%fused_computation.5 | loop fusion | flops 655360 | bytes 2621568 | tf_op jit(solution)/shard_map/jit(_take)/select_n | solution.py:206
  66.3 10.7 %all-to-all-start = ((bf16[128,2,10,256]{3,1,2,0:T(2,128)(2,1)}), bf16[128,2,10,256]{3,1,2,0:T(2,128)(2,1)S(1)}, u32[]{:S(2)}, u32[]{:S(2)}) async-start(bf16[128,2,10,256]{3,1,2,0:T(2,128)(2,1)} %broadcast_select_fusion.1), calls=%async_computation | async-start | bytes 2621440 | tf_op jit(solution)/shard_map/all_to_all | solution.py:207
  77.0 0.0 copy-done.2
  77.1 34.1 %all-to-all-done = bf16[128,2,10,256]{3,1,2,0:T(2,128)(2,1)S(1)} async-done(((bf16[128,2,10,256]{3,1,2,0:T(2,128)(2,1)}), bf16[128,2,10,256]{3,1,2,0:T(2,128)(2,1)S(1)}, u32[]{:S(2)}, u32[]{:S(2)}) %all-to-all-start) | async-done | bytes 1310752 | tf_op jit(solution)/shard_map/all_to_all | solution.py:207
  111.2 0.9 copy.21
  112.1 0.0 copy-start
  112.1 0.0 copy-start.1
  112.1 1.5 reshape.27
  113.6 1.5 copy.12.four_ref
  115.1 0.0 copy-done
  115.1 0.0 copy-done.1
  115.1 105.7 %shard_map.64 = bf16[2,5136,256]{2,1,0:T(8,128)(2,1)} custom-call(bf16[4,640,256]{2,1,0:T(8,128)(2,1)S(1)} %copy.12.four_ref, s32[1,640]{1,0:T(1,128)S(1)} %broadcast_in_dim.44.wave_ref, s32[1,256]{1,0:T(1,128)S(1)} %bitcast.24, s32[1,256]{1,0:T(1,128)S(1)} %bitcast.25), custom_call_target="tpu_custom_call" | custom-call | flops 8053063680 | bytes 7340032 | tf_op jit(solution)/shard_map/pallas_call | solution.py:170
  (2 shorter events, 0.0 us)
Async XLA Ops:
  6.5 49.6 %all-gather.2.cloned.1.call-start = ((), (), s32[]{:S(2)}) async-start(), calls=%async_computation.1 | async-start | bytes 4096000 | tf_op jit(solution)/shard_map/all_gather | solution.py:203
  63.9 13.1 %copy-start.2 = (s32[640]{0:T(1024)S(1)}, s32[640]{0:T(1024)}, u32[]{:S(2)}) copy-start(s32[640]{0:T(1024)} %param.8) | copy-start | bytes 7684
  66.3 44.9 %all-to-all-start = ((bf16[128,2,10,256]{3,1,2,0:T(2,128)(2,1)}), bf16[128,2,10,256]{3,1,2,0:T(2,128)(2,1)S(1)}, u32[]{:S(2)}, u32[]{:S(2)}) async-start(bf16[128,2,10,256]{3,1,2,0:T(2,128)(2,1)} %broadcast_select_fusion.1), calls=%async_computation | async-start | bytes 2621440 | tf_op jit(solution)/shard_map/all_to_all | solution.py:207
  112.1 3.0 %copy-start = (s32[256]{0:T(256)S(1)}, s32[256]{0:T(256)}, u32[]{:S(2)}) copy-start(s32[256]{0:T(256)} %param.9) | copy-start | bytes 3076
  112.1 3.0 %copy-start.1 = (s32[256]{0:T(256)S(1)}, s32[256]{0:T(256)}, u32[]{:S(2)}) copy-start(s32[256]{0:T(256)} %param.10) | copy-start | bytes 3076
Sparse Core Ops, SparseCore 0:
  9.2 46.9 all-gather.1

commit v2 on v1

--- a/solution.py
+++ b/solution.py
@@ -42,7 +42,7 @@
 
 def zonal_kernel(
     four_ref, wave_ref, points_ref, slot_ref, out_ref,
-    live, npts, inner_c, inner_s, step_c, step_s, outer_c, outer_s, lead_r, lead_i, left, table, rows,
+    live, npts, place, inner_c, inner_s, step_c, step_s, outer_c, outer_s, lead_r, lead_i, left, table, rows,
 ):
     lat = slot_ref.shape[1]
     waves = wave_ref.shape[1]
@@ -51,20 +51,22 @@
     blocks = pl.cdiv(lon, LANES)
     bf16, f32 = jnp.bfloat16, jnp.float32
 
-    held = lax.broadcasted_iota(jnp.int32, (lat, lat), 0)
-    by_lane = jnp.where(held == slot_ref[...], 1.0, 0.0).astype(bf16)
-    eye = jnp.where(held == lax.broadcasted_iota(jnp.int32, (lat, lat), 1), 1.0, 0.0).astype(bf16)
-    chosen = dot_nt(eye, by_lane)
-    npts[...] = jnp.broadcast_to(
-        jnp.sum(chosen * points_ref[...].astype(f32), axis=1, keepdims=True), (lat, LANES)
-    )
-    chosen = chosen.astype(bf16)
+    row_i = lax.broadcasted_iota(jnp.int32, (lat, lat), 0)
+    eye = jnp.where(row_i == lax.broadcasted_iota(jnp.int32, (lat, lat), 1), 1.0, 0.0)
+    count = points_ref[...].astype(f32)
+    count_down = jnp.sum(eye * count, axis=1, keepdims=True)
+    rank = jnp.sum(jnp.where(count_down < count, 1.0, 0.0), axis=0, keepdims=True)
+    order = jnp.where(row_i.astype(f32) == rank, 1.0, 0.0)
+    npts[...] = jnp.broadcast_to(jnp.sum(order * count, axis=1, keepdims=True), (lat, LANES))
+    order = order.astype(bf16)
+    in_slot = jnp.where(row_i == slot_ref[...], 1.0, 0.0).astype(bf16)
+    place[...] = jnp.dot(order, in_slot, preferred_element_type=f32).astype(bf16)
     for part in range(4):
-        moved = dot_nt(chosen, four_ref[part])
+        moved = dot_nt(order, four_ref[part])
         for t in range(tiles):
             live[part, t] = moved[:, t * LANES:(t + 1) * LANES]
 
-    def block(i, carry):
+    def block(i, carry, far_count):
         s0 = pl.multiple_of(i * SUBLANES, SUBLANES)
         points = npts[pl.ds(s0, SUBLANES), :]
         inverse = 1.0 / points
@@ -80,8 +82,8 @@
                 step_s[t, pl.ds(j * 8, 8), :] = s
             for j, (c, s) in enumerate(powers(turn(m * 128.0, points, inverse), 8)):
                 outer_c[t, pl.ds(j * 8, 8), :] = c
-                outer_s[t, pl.ds(j * 8, 8), :] = s
-            far = powers(turn(m * 1024.0, points, inverse), COARSE // 8)
+                outer_s[t, pl.ds(j * 8, 8), :] = -s
+            far = powers(turn(m * 1024.0, points, inverse), far_count)
             for p in range(2):
                 value = (
                     live[2 * p, t, pl.ds(s0, SUBLANES), :] * weight,
@@ -90,11 +92,10 @@
                 value = times(value, steps[8])
                 for a, w in enumerate(far):
                     r, im = times(value, w) if a else value
-                    row = (p * (COARSE // 8) + a) * 8
-                    lead_r[t, pl.ds(row, 8), :] = r
-                    lead_i[t, pl.ds(row, 8), :] = im
-
-        def one(l, buf):
+                    lead_r[t, pl.ds((a * 2 + p) * 8, 8), :] = r
+                    lead_i[t, pl.ds((a * 2 + p) * 8, 8), :] = im
+
+        def make(l, buf):
             def bcast(ref, t, row):
                 return ref[t, pl.ds(row * 8 + l, 8, stride=0), :]
 
@@ -119,43 +120,58 @@
                     table[buf, pl.ds(q * 16, 16), there] = jnp.concatenate(
                         [ss[2 * q], ss[2 * q + 1]], axis=0).astype(bf16)
                 oc, os = spread(outer_c, t), spread(outer_s, t)
-                for q in range(COARSE // 8):
+                for q in range(far_count):
                     res, ims = [], []
                     for h in range(2):
                         fr, fi = bcast(lead_r, t, 2 * q + h), bcast(lead_i, t, 2 * q + h)
-                        res.append(fr * oc - fi * os)
-                        ims.append(-(fr * os) - fi * oc)
+                        res.append(fr * oc + fi * os)
+                        ims.append(fr * os - fi * oc)
                     left[buf, pl.ds(q * 16, 16), here] = jnp.concatenate(res, axis=0).astype(bf16)
                     left[buf, pl.ds(q * 16, 16), there] = jnp.concatenate(ims, axis=0).astype(bf16)
-            rows[pl.ds(s0 + l, 2 * COARSE, stride=lat), :] = dot_nt(left[buf], table[buf])
-
-        def pair(h, carry):
-            one(2 * h, 0)
-            one(2 * h + 1, 1)
-            return carry
-
-        return lax.fori_loop(0, SUBLANES // 2, pair, carry)
-
-    lax.fori_loop(0, lat // SUBLANES, block, 0)
-
-    small = eye[:LANES, :LANES]
+
+        def multiply(l, buf):
+            rows[pl.ds(s0 + l, 16 * far_count, stride=lat), :] = dot_nt(
+                left[buf, :16 * far_count], table[buf])
+
+        make(0, 0)
+        for l in range(1, SUBLANES):
+            make(l, l % 2)
+            multiply(l - 1, (l - 1) % 2)
+        multiply(SUBLANES - 1, (SUBLANES - 1) % 2)
+        return carry
+
+    start = 0
+    for far_count in range(2, COARSE // 8 + 1, 2):
+        if far_count == COARSE // 8:
+            end = lat // SUBLANES
+        else:
+            fits = jnp.where(count <= far_count * 1024.0, 1.0, 0.0)
+            end = jnp.sum(fits).astype(jnp.int32) // SUBLANES
+        lax.fori_loop(start, end, functools.partial(block, far_count=far_count), 0)
+        start = end
+
+    small = eye[:LANES, :LANES].astype(bf16)
     lane = lax.broadcasted_iota(jnp.int32, (lat, LANES), 1).astype(f32)
 
     def turned(p, a):
-        start = pl.multiple_of((p * COARSE + a) * lat, lat)
-        value = rows[pl.ds(start, lat), :]
+        at = (a // 8) * 16 + p * 8 + a % 8
+        value = rows[pl.ds(pl.multiple_of(at * lat, lat), lat), :]
         first = jnp.float32(a * LANES) if isinstance(a, int) else (a * LANES).astype(f32)
         value = jnp.where(lane + first < npts[...], value, 0.0).astype(bf16)
-        return dot_nt(small, value).astype(bf16)
+        value = dot_nt(small, value).astype(bf16)
+        return jnp.dot(value, place[...], preferred_element_type=f32).astype(bf16)
 
     for p in range(2):
-        def whole(a, carry, p=p):
-            out_ref[p, pl.ds(pl.multiple_of(a * LANES, LANES), LANES), :] = turned(p, a)
+        def whole(h, carry, p=p):
+            for a in (2 * h, 2 * h + 1):
+                out_ref[p, pl.ds(pl.multiple_of(a * LANES, LANES), LANES), :] = turned(p, a)
             return carry
 
-        lax.fori_loop(0, blocks - 1, whole, 0)
-        last = (blocks - 1) * LANES
-        out_ref[p, last:, :] = turned(p, blocks - 1)[:lon - last]
+        lax.fori_loop(0, (blocks - 1) // 2, whole, 0)
+        for a in range((blocks - 1) // 2 * 2, blocks):
+            first = a * LANES
+            size = min(LANES, lon - first)
+            out_ref[p, first:first + size, :] = turned(p, a)[:size]
 
 
 def zonal(four, wave_of_row, row_points, lat_slot, lon):
@@ -175,6 +191,7 @@
         scratch_shapes=[
             pltpu.VMEM((4, tiles, lat, LANES), f32),
             pltpu.VMEM((lat, LANES), f32),
+            pltpu.VMEM((lat, lat), jnp.bfloat16),
             scratch(8), scratch(8), scratch(9), scratch(9), scratch(8), scratch(8),
             scratch(2 * COARSE // 8), scratch(2 * COARSE // 8),
             pltpu.VMEM((2, 2 * COARSE, 2 * waves), jnp.bfloat16),

time: 228 us -> 212 us (0.930)
  Pallas kernels: 106 us -> 89.7 us
    pallas_call x1, Pallas kernels: 106 us -> 89.7 us  [zonal(): pl.pallas_call(zonal_kernel, out_shape=jax.ShapeDtypeStruct((2, lon, lat)...]
where the time goes in v2:
time: 212 us
  Pallas kernels  89.7 us (42%)
  waiting for transfers between devices  76.9 us (36%)
  between operations  13.5 us (6%)
  starting transfers between devices  10.7 us (5%)
  local copies, waits for them, and re-layouts  9.26 us (4%)
  other arithmetic  8.51 us (4%)
  matrix products  3.15 us (1%)
    pallas_call x1, Pallas kernels, zonal(): pl.pallas_call(zonal_kernel, out_shape=jax.ShapeDtypeStruct((2, lon, lat)...  89.7 us
    all_gather x1, waiting for transfers between devices, local(): lax.all_gather(legendre, 'fld', axis=2, tiled=True)  42 us
    all_to_all x1, waiting for transfers between devices, local(): lax.all_to_all(fourier, 'wave', split_axis=0, concat_axis=2, tiled=True)  34.1 us
    all_to_all x1, starting transfers between devices, local(): lax.all_to_all(fourier, 'wave', split_axis=0, concat_axis=2, tiled=True)  10.7 us
    select_n x1, other arithmetic, local(): jnp.where(alive_mask[None, None], spectral[0], jnp.zeros((), jnp.bfloat16))  4.72 us
  transfers between devices with their start and end apart: 2, of which 2 were waited for; matrix products, arithmetic and copies ran while one was open for 3% of the time, Pallas kernels for 0%

profile of v2, /device:TPU:1, one launch (start us, length us, event | category | flops | bytes accessed | tf_op | source)
XLA Modules:
  0.0 211.7 jit_solution(13146834493312254530)
XLA Ops:
  6.5 0.0 all-gather.2.cloned.1.call-start
  6.5 0.7 all-gather.2.cloned.1.call-update
  7.3 0.8 dynamic_slice.3
  8.0 0.7 compare_select_fusion
  8.7 0.7 compare_and_fusion
  9.4 0.1 iota_compare_fusion
  9.4 4.7 %broadcast_select_fusion = bf16[128,2,10,640]{3,1,2,0:T(2,128)(2,1)S(1)} fusion(pred[10,640]{1,0:T(8,128)(4,1)S(1)} %iota_compare_fusion, bf16[1,128,2,10,640]{4,2,3,1,0:T(2,128)(2,1)} %param.6), kind=kLoop, calls=%fused_computation.1 | loop fusion | flops 1638400 | bytes 6560000 | tf_op jit(solution)/shard_map/jit(_where)/select_n | solution.py:216
  14.2 42.0 %all-gather.2.cloned.1.call-done = bf16[10,640,256]{1,2,0:T(8,128)(2,1)} async-done(((bf16[10,640,64]{1,2,0:T(8,128)(2,1)}), bf16[10,640,256]{1,2,0:T(8,128)(2,1)}) %all-gather.2.cloned.1.call-update) | async-done | bytes 3276816 | tf_op jit(solution)/shard_map/all_gather | solution.py:220
  56.2 3.1 %fusion.8 = bf16[128,2,10,256]{3,0,1,2:T(8,128)(2,1)S(1)} fusion(bf16[10,640,256]{1,2,0:T(8,128)(2,1)} %all-gather.2.cloned.1.call-done, bf16[128,2,10,640]{3,1,2,0:T(2,128)(2,1)S(1)} %broadcast_select_fusion), kind=kOutput, calls=%fused_computation.7 | convolution fusion | flops 839516160 | bytes 7864320 | tf_op jit(solution)/shard_map/pcrn,rnj->pcrj/dot_general | solution.py:217
  59.3 1.3 copy.10
  60.7 3.2 %gather_fusion = bf16[128,2,10,256]{3,1,2,0:T(2,128)(2,1)S(1)} fusion(bf16[128,2,10,256]{3,1,2,0:T(2,128)(2,1)S(1)} %copy.10, s32[1024]{0:T(1024)S(1)} %pad_clamp_fusion), kind=kCustom, calls=%fused_computation | custom fusion | bytes 2621952 | tf_op jit(solution)/shard_map/jit(_take)/gather | solution.py:223
  63.9 0.0 copy-start.2
  63.9 2.4 %broadcast_select_fusion.1 = bf16[128,2,10,256]{3,1,2,0:T(2,128)(2,1)} fusion(bf16[128,2,10,256]{3,1,2,0:T(2,128)(2,1)S(1)} %gather_fusion, pred[128]{0:T(512)(128)(4,1)S(1)} %compare_and_fusion), kind=kLoop, calls=%fused_computation.5 | loop fusion | flops 655360 | bytes 2621568 | tf_op jit(solution)/shard_map/jit(_take)/select_n | solution.py:223
  66.3 10.7 %all-to-all-start = ((bf16[128,2,10,256]{3,1,2,0:T(2,128)(2,1)}), bf16[128,2,10,256]{3,1,2,0:T(2,128)(2,1)S(1)}, u32[]{:S(2)}, u32[]{:S(2)}) async-start(bf16[128,2,10,256]{3,1,2,0:T(2,128)(2,1)} %broadcast_select_fusion.1), calls=%async_computation | async-start | bytes 2621440 | tf_op jit(solution)/shard_map/all_to_all | solution.py:224
  77.0 0.0 copy-done.2
  77.1 34.1 %all-to-all-done = bf16[128,2,10,256]{3,1,2,0:T(2,128)(2,1)S(1)} async-done(((bf16[128,2,10,256]{3,1,2,0:T(2,128)(2,1)}), bf16[128,2,10,256]{3,1,2,0:T(2,128)(2,1)S(1)}, u32[]{:S(2)}, u32[]{:S(2)}) %all-to-all-start) | async-done | bytes 1310752 | tf_op jit(solution)/shard_map/all_to_all | solution.py:224
  111.2 0.9 copy.21
  112.1 0.0 copy-start
  112.1 0.0 copy-start.1
  112.1 1.5 reshape.27
  113.6 1.5 copy.12.four_ref
  115.1 0.0 copy-done
  115.1 0.0 copy-done.1
  115.2 89.7 %shard_map.64 = bf16[2,5136,256]{2,1,0:T(8,128)(2,1)} custom-call(bf16[4,640,256]{2,1,0:T(8,128)(2,1)S(1)} %copy.12.four_ref, s32[1,640]{1,0:T(1,128)S(1)} %broadcast_in_dim.44.wave_ref, s32[1,256]{1,0:T(1,128)S(1)} %bitcast.24, s32[1,256]{1,0:T(1,128)S(1)} %bitcast.25), custom_call_target="tpu_custom_call" | custom-call | flops 8053063680 | bytes 7340032 | tf_op jit(solution)/shard_map/pallas_call | solution.py:186
  (2 shorter events, 0.0 us)
Async XLA Ops:
  6.5 49.6 %all-gather.2.cloned.1.call-start = ((), (), s32[]{:S(2)}) async-start(), calls=%async_computation.1 | async-start | bytes 4096000 | tf_op jit(solution)/shard_map/all_gather | solution.py:220
  63.9 13.1 %copy-start.2 = (s32[640]{0:T(1024)S(1)}, s32[640]{0:T(1024)}, u32[]{:S(2)}) copy-start(s32[640]{0:T(1024)} %param.8) | copy-start | bytes 7684
  66.3 44.9 %all-to-all-start = ((bf16[128,2,10,256]{3,1,2,0:T(2,128)(2,1)}), bf16[128,2,10,256]{3,1,2,0:T(2,128)(2,1)S(1)}, u32[]{:S(2)}, u32[]{:S(2)}) async-start(bf16[128,2,10,256]{3,1,2,0:T(2,128)(2,1)} %broadcast_select_fusion.1), calls=%async_computation | async-start | bytes 2621440 | tf_op jit(solution)/shard_map/all_to_all | solution.py:224
  112.1 3.0 %copy-start = (s32[256]{0:T(256)S(1)}, s32[256]{0:T(256)}, u32[]{:S(2)}) copy-start(s32[256]{0:T(256)} %param.9) | copy-start | bytes 3076
  112.1 3.0 %copy-start.1 = (s32[256]{0:T(256)S(1)}, s32[256]{0:T(256)}, u32[]{:S(2)}) copy-start(s32[256]{0:T(256)} %param.10) | copy-start | bytes 3076
Sparse Core Ops, SparseCore 0:
  9.2 46.9 all-gather.1

commit v3 on v2

--- a/solution.py
+++ b/solution.py
@@ -10,6 +10,7 @@
 
 LANES = 128
 SUBLANES = 8
+MESSAGE = 16
 COARSE = 48
 
 
@@ -42,7 +43,7 @@
 
 def zonal_kernel(
     four_ref, wave_ref, points_ref, slot_ref, out_ref,
-    live, npts, place, inner_c, inner_s, step_c, step_s, outer_c, outer_s, lead_r, lead_i, left, table, rows,
+    live, npts, place, wide, held, inner_c, inner_s, step_c, step_s, outer_c, outer_s, lead_r, lead_i, left, table, rows,
 ):
     lat = slot_ref.shape[1]
     waves = wave_ref.shape[1]
@@ -61,8 +62,16 @@
     order = order.astype(bf16)
     in_slot = jnp.where(row_i == slot_ref[...], 1.0, 0.0).astype(bf16)
     place[...] = jnp.dot(order, in_slot, preferred_element_type=f32).astype(bf16)
+    sources = four_ref.shape[1] // MESSAGE
+    for chunk in range(four_ref.shape[0]):
+        wide[...] = four_ref[chunk].astype(f32)
+        for part in range(4):
+            for r in range(2):
+                halves = [wide[pl.ds(part * 4 + r * 2 + h, sources, stride=MESSAGE), :] for h in range(2)]
+                held[part, pl.ds((chunk * 2 + r) * sources, sources), :] = jnp.concatenate(
+                    halves, axis=1).astype(bf16)
     for part in range(4):
-        moved = dot_nt(order, four_ref[part])
+        moved = dot_nt(order, held[part])
         for t in range(tiles):
             live[part, t] = moved[:, t * LANES:(t + 1) * LANES]
 
@@ -73,23 +82,27 @@
         for t in range(tiles):
             m = jnp.broadcast_to(wave_ref[:, t * LANES:(t + 1) * LANES].astype(f32), points.shape)
             weight = jnp.where(2.0 * m < points, jnp.where(m == 0.0, 1.0, 2.0), 0.0)
-            for j, (c, s) in enumerate(powers(turn(m, points, inverse), 8)):
-                inner_c[t, pl.ds(j * 8, 8), :] = c
-                inner_s[t, pl.ds(j * 8, 8), :] = s
-            steps = powers(turn(m * 8.0, points, inverse), 9)
+            half = turn(m, 2.0 * points, 0.5 * inverse)
+            steps = powers(turn(m * 8.0, points, inverse), 5)
             for j, (c, s) in enumerate(steps):
                 step_c[t, pl.ds(j * 8, 8), :] = c
                 step_s[t, pl.ds(j * 8, 8), :] = s
+            middle = times(half, steps[4])
+            for j, w in enumerate(powers(times(half, half), 8)):
+                c, s = times(middle, w) if j else middle
+                inner_c[t, pl.ds(j * 8, 8), :] = c
+                inner_s[t, pl.ds(j * 8, 8), :] = s
+            centre = times(times(steps[4], steps[4]), (half[0], -half[1]))
             for j, (c, s) in enumerate(powers(turn(m * 128.0, points, inverse), 8)):
                 outer_c[t, pl.ds(j * 8, 8), :] = c
-                outer_s[t, pl.ds(j * 8, 8), :] = -s
+                outer_s[t, pl.ds(j * 8, 8), :] = s
             far = powers(turn(m * 1024.0, points, inverse), far_count)
             for p in range(2):
                 value = (
                     live[2 * p, t, pl.ds(s0, SUBLANES), :] * weight,
                     live[2 * p + 1, t, pl.ds(s0, SUBLANES), :] * weight,
                 )
-                value = times(value, steps[8])
+                value = times(value, centre)
                 for a, w in enumerate(far):
                     r, im = times(value, w) if a else value
                     lead_r[t, pl.ds((a * 2 + p) * 8, 8), :] = r
@@ -104,17 +117,17 @@
 
             for t in range(tiles):
                 ic, isn = spread(inner_c, t), spread(inner_s, t)
-                cs, ss = [None] * 16, [None] * 16
-                cs[8], ss[8] = ic, isn
-                for j in range(1, 9):
+                cs, ss = [None] * 8, [None] * 8
+                cs[4], ss[4] = ic, isn
+                for j in range(1, 5):
                     wc, ws = bcast(step_c, t, j), bcast(step_s, t, j)
                     a, b, c, d = ic * wc, isn * ws, isn * wc, ic * ws
-                    if j < 8:
-                        cs[8 + j], ss[8 + j] = a - b, c + d
-                    cs[8 - j], ss[8 - j] = a + b, c - d
+                    if j < 4:
+                        cs[4 + j], ss[4 + j] = a - b, c + d
+                    cs[4 - j], ss[4 - j] = a + b, c - d
                 here = pl.ds(t * LANES, LANES)
                 there = pl.ds(waves + t * LANES, LANES)
-                for q in range(8):
+                for q in range(4):
                     table[buf, pl.ds(q * 16, 16), here] = jnp.concatenate(
                         [cs[2 * q], cs[2 * q + 1]], axis=0).astype(bf16)
                     table[buf, pl.ds(q * 16, 16), there] = jnp.concatenate(
@@ -124,14 +137,17 @@
                     res, ims = [], []
                     for h in range(2):
                         fr, fi = bcast(lead_r, t, 2 * q + h), bcast(lead_i, t, 2 * q + h)
-                        res.append(fr * oc + fi * os)
-                        ims.append(fr * os - fi * oc)
+                        res.append(fr * oc - fi * os)
+                        ims.append(fr * os + fi * oc)
                     left[buf, pl.ds(q * 16, 16), here] = jnp.concatenate(res, axis=0).astype(bf16)
                     left[buf, pl.ds(q * 16, 16), there] = jnp.concatenate(ims, axis=0).astype(bf16)
 
         def multiply(l, buf):
-            rows[pl.ds(s0 + l, 16 * far_count, stride=lat), :] = dot_nt(
-                left[buf, :16 * far_count], table[buf])
+            used = pl.ds(0, 16 * far_count)
+            even = dot_nt(left[buf, used, :waves], table[buf, :, :waves])
+            odd = dot_nt(left[buf, used, waves:], table[buf, :, waves:])
+            rows[pl.ds(s0 + l, 16 * far_count, stride=lat), :] = jnp.concatenate(
+                [even - odd, even + odd], axis=1)
 
         make(0, 0)
         for l in range(1, SUBLANES):
@@ -150,8 +166,13 @@
         lax.fori_loop(start, end, functools.partial(block, far_count=far_count), 0)
         start = end
 
-    small = eye[:LANES, :LANES].astype(bf16)
-    lane = lax.broadcasted_iota(jnp.int32, (lat, LANES), 1).astype(f32)
+    def longitude_of(shape):
+        lane = lax.broadcasted_iota(jnp.int32, shape, 1)
+        return jnp.where(lane < LANES // 2, lane + LANES // 2, LANES - 1 - lane)
+
+    square = (LANES, LANES)
+    small = jnp.where(lax.broadcasted_iota(jnp.int32, square, 0) == longitude_of(square), 1.0, 0.0).astype(bf16)
+    lane = longitude_of((lat, LANES)).astype(f32)
 
     def turned(p, a):
         at = (a // 8) * 16 + p * 8 + a % 8
@@ -175,7 +196,7 @@
 
 
 def zonal(four, wave_of_row, row_points, lat_slot, lon):
-    _, waves, lat = four.shape
+    waves, lat = wave_of_row.shape[0], lat_slot.shape[0]
     tiles = waves // LANES
     f32 = jnp.float32
     vmem = pl.BlockSpec(memory_space=pltpu.VMEM)
@@ -192,10 +213,12 @@
             pltpu.VMEM((4, tiles, lat, LANES), f32),
             pltpu.VMEM((lat, LANES), f32),
             pltpu.VMEM((lat, lat), jnp.bfloat16),
-            scratch(8), scratch(8), scratch(9), scratch(9), scratch(8), scratch(8),
+            pltpu.VMEM(four.shape[1:], f32),
+            pltpu.VMEM((4, waves, lat), jnp.bfloat16),
+            scratch(8), scratch(8), scratch(5), scratch(5), scratch(8), scratch(8),
             scratch(2 * COARSE // 8), scratch(2 * COARSE // 8),
             pltpu.VMEM((2, 2 * COARSE, 2 * waves), jnp.bfloat16),
-            pltpu.VMEM((2, LANES, 2 * waves), jnp.bfloat16),
+            pltpu.VMEM((2, LANES // 2, 2 * waves), jnp.bfloat16),
             pltpu.VMEM((2 * COARSE * lat, LANES), f32),
         ],
         compiler_params=pltpu.CompilerParams(vmem_limit_bytes=48 * 1024 * 1024),
@@ -206,24 +229,174 @@
 
 
 LON = 5136
+MESH = pl.DeviceIdType.MESH
+
+
+def spectral_kernel(
+    spec_ref, leg_ref, wave_ref, field_ref, recv_ref,
+    legs, swap, mixed, outbox,
+    own_sem, send_a, recv_a, send_f, recv_f, send_m, recv_m, keep_m,
+):
+    bf16, f32 = jnp.bfloat16, jnp.float32
+    me, y = lax.axis_index("wave"), lax.axis_index("fld")
+    peers, ring = lax.axis_size("wave"), lax.axis_size("fld")
+    right, left = lax.rem(y + 1, ring), lax.rem(y + ring - 1, ring)
+    rows_here, lats_here, degrees = leg_ref.shape
+    chunks = rows_here // 2
+    pairs = spec_ref.shape[1]
+
+    def there(k):
+        return lax.rem(me + k, peers)
+
+    barrier = pltpu.get_barrier_semaphore()
+
+    def greet(k, carry):
+        pl.semaphore_signal(barrier, inc=1, device_id=(there(k), y), device_id_type=MESH)
+        return carry
+
+    for side in (right, left):
+        pl.semaphore_signal(barrier, inc=1, device_id=(me, side), device_id_type=MESH)
+    lax.fori_loop(1, peers, greet, 0)
+
+    def own():
+        return pltpu.make_async_copy(leg_ref, legs.at[y], own_sem)
+
+    def first(c, side):
+        at = pl.ds(2 * c, 2)
+        return pltpu.make_async_remote_copy(
+            src_ref=leg_ref.at[at], dst_ref=legs.at[y, at],
+            send_sem=send_a.at[side, c], recv_sem=recv_a.at[side, c],
+            device_id=(me, (right, left)[side]), device_id_type=MESH)
+
+    def second(c, side):
+        block, at = (left, right)[side], pl.ds(2 * c + side, 1)
+        return pltpu.make_async_remote_copy(
+            src_ref=legs.at[block, at], dst_ref=legs.at[block, at],
+            send_sem=send_f.at[side, c], recv_sem=recv_f.at[side, c],
+            device_id=(me, (right, left)[side]), device_id_type=MESH)
+
+    def message(c, k):
+        return pltpu.make_async_remote_copy(
+            src_ref=outbox.at[c, there(k)], dst_ref=recv_ref.at[c, me],
+            send_sem=send_m.at[c], recv_sem=recv_m.at[c],
+            device_id=(there(k), y), device_id_type=MESH)
+
+    def all_messages(c):
+        some = pl.ds(0, peers - 1)
+        return pltpu.make_async_remote_copy(
+            src_ref=outbox.at[c, some], dst_ref=recv_ref.at[c, some],
+            send_sem=send_m.at[c], recv_sem=recv_m.at[c],
+            device_id=(there(1), y), device_id_type=MESH)
+
+    def kept(c):
+        return pltpu.make_async_copy(outbox.at[c, me], recv_ref.at[c, me], keep_m.at[c])
+
+    own().start()
+
+    row_i = lax.broadcasted_iota(jnp.int32, (pairs, pairs), 0)
+    col_i = lax.broadcasted_iota(jnp.int32, (pairs, pairs), 1)
+    eye = jnp.where(row_i == col_i, 1.0, 0.0).astype(bf16)
+    twice_i = lax.broadcasted_iota(jnp.int32, (pairs // 2, pairs), 1)
+    twice = jnp.where(
+        lax.broadcasted_iota(jnp.int32, (pairs // 2, pairs), 0) == twice_i // 2, 1.0, 0.0).astype(bf16)
+    fields = jnp.broadcast_to(field_ref[...].astype(f32), (8, pairs // 2)).astype(bf16)
+    wanted = 2.0 * jnp.dot(fields, twice, preferred_element_type=f32)[0:1]
+    wanted = wanted + (col_i[0:1] % 2).astype(f32)
+    swap[...] = dot_nt(eye, jnp.where(row_i.astype(f32) == wanted, 1.0, 0.0).astype(bf16)).astype(bf16)
+
+    own().wait()
+    pl.semaphore_wait(barrier, peers + 1)
+    for c in range(3):
+        for side in range(2):
+            first(c, side).start()
+
+    def pass_on(c):
+        for side in range(2):
+            first(c, side).wait_recv()
+        for side in range(2):
+            second(c, side).start()
+
+    pass_on(0)
+
+    def step(c, carry):
+        @pl.when(c < chunks - 1)
+        def _():
+            pass_on(c + 1)
+
+        @pl.when(c < chunks - 3)
+        def _():
+            for side in range(2):
+                first(c + 3, side).start()
+
+        for side in range(2):
+            second(c, side).wait_recv()
+        degree = lax.broadcasted_iota(jnp.int32, (ring * lats_here, degrees), 1)
+        for r in range(2):
+            row = 2 * c + r
+            values = jnp.concatenate([legs[g, row] for g in range(ring)], axis=0)
+            values = jnp.where(degree >= wave_ref[me * rows_here + row], values.astype(f32), 0.0).astype(bf16)
+            fourier = dot_nt(spec_ref[row], values).astype(bf16)
+            fourier = jnp.dot(swap[...], fourier, preferred_element_type=f32)
+            for h in range(2):
+                mixed[pl.ds(r * 2 + h, pairs, stride=4), :] = fourier[:, h * LANES:(h + 1) * LANES]
+        outbox[c] = mixed[...].astype(bf16).reshape(outbox.shape[1:])
+        kept(c).start()
+
+        def post(k, carry):
+            message(c, k).start()
+            return carry
+
+        return lax.fori_loop(1, peers, post, carry)
+
+    lax.fori_loop(0, chunks, step, 0)
+
+    def finish(c, carry):
+        for side in range(2):
+            first(c, side).wait_send()
+            second(c, side).wait_send()
+        kept(c).wait()
+        all_messages(c).wait()
+        return carry
+
+    lax.fori_loop(0, chunks, finish, 0)
+
+
+def spectral_part(spec, legendre, wave_of_row, field_slot, peers, ring):
+    rows_here, pairs, degrees = spec.shape
+    lats_here = legendre.shape[1]
+    chunks = rows_here // 2
+    bf16 = jnp.bfloat16
+    vmem = pl.BlockSpec(memory_space=pltpu.VMEM)
+    pairs_sem = pltpu.SemaphoreType.DMA((2, chunks))
+    chunk_sem = pltpu.SemaphoreType.DMA((chunks,))
+    return pl.pallas_call(
+        spectral_kernel,
+        out_shape=jax.ShapeDtypeStruct((chunks, peers, MESSAGE, LANES), bf16),
+        in_specs=[vmem, vmem, pl.BlockSpec(memory_space=pltpu.SMEM), vmem],
+        out_specs=pl.BlockSpec(memory_space=pl.ANY),
+        scratch_shapes=[
+            pltpu.VMEM((ring, rows_here, lats_here, degrees), bf16),
+            pltpu.VMEM((pairs, pairs), bf16),
+            pltpu.VMEM((peers * MESSAGE, LANES), jnp.float32),
+            pltpu.VMEM((chunks, peers, MESSAGE, LANES), bf16),
+            pltpu.SemaphoreType.DMA,
+            pairs_sem, pairs_sem, pairs_sem, pairs_sem, chunk_sem, chunk_sem, chunk_sem,
+        ],
+        compiler_params=pltpu.CompilerParams(
+            collective_id=0, has_side_effects=True, vmem_limit_bytes=40 * 1024 * 1024),
+        cost_estimate=pl.CostEstimate(
+            flops=2 * rows_here * pairs * degrees * lats_here * ring, bytes_accessed=6 << 20, transcendentals=0),
+    )(spec, legendre, wave_of_row, field_slot[None])
 
 
 def local(spectral, legendre, wave_of_row, row_points, lat_slot, field_slot):
     rows_here, degree_count, _ = legendre.shape
-    my_waves = lax.dynamic_slice_in_dim(wave_of_row, lax.axis_index("wave") * rows_here, rows_here)
-    degrees = jnp.arange(degree_count, dtype=jnp.int32)
-    alive_mask = degrees[None, :] >= my_waves[:, None]
-    masked = jnp.where(alive_mask[None, None], spectral[0], jnp.zeros((), jnp.bfloat16))
-    fourier = jnp.einsum(
-        "pcrn,rnj->pcrj",
-        masked,
-        lax.all_gather(legendre, "fld", axis=2, tiled=True),
-        preferred_element_type=jnp.float32,
-    ).astype(jnp.bfloat16)
-    fourier = jnp.take(fourier, field_slot, axis=0)
-    fourier = lax.all_to_all(fourier, "wave", split_axis=0, concat_axis=2, tiled=True)
-    fourier = fourier.reshape(4, -1, lat_slot.shape[0])
-    grid = zonal(fourier, wave_of_row, row_points, lat_slot, LON)
+    peers, ring = lax.axis_size("wave"), lax.axis_size("fld")
+    spec = jnp.transpose(spectral[0], (2, 0, 1, 3)).reshape(rows_here, -1, degree_count)
+    four = spectral_part(spec, jnp.transpose(legendre, (0, 2, 1)), wave_of_row, field_slot, peers, ring)
+    four = four.reshape(rows_here // 2, peers * MESSAGE, LANES)
+    waves = wave_of_row.reshape(peers, rows_here).T.reshape(-1)
+    grid = zonal(four, waves, row_points, lat_slot, LON)
     return jnp.transpose(grid, (0, 2, 1))[None]
 
 

time: 212 us -> 148 us (0.70)
  waiting for transfers between devices: 76.9 us -> 0 us
  Pallas kernels: 89.7 us -> 133 us
  between operations: 13.5 us -> 0.07 us
  starting transfers between devices: 10.7 us -> 0 us
  other arithmetic: 8.51 us -> 0 us
  local copies, waits for them, and re-layouts: 9.26 us -> 15 us
  matrix products: 3.15 us -> 0 us
    pallas_call x0 -> x1, Pallas kernels: none -> 59.6 us  [spectral_part(): pl.pallas_call(spectral_kernel, out_shape=jax.ShapeDtypeStruct((chunks, p...]
    all_gather x1 -> x0, waiting for transfers between devices: 42 us -> none  [local(): lax.all_gather(legendre, 'fld', axis=2, tiled=True)]
    all_to_all x1 -> x0, waiting for transfers between devices: 34.1 us -> none  [local(): lax.all_to_all(fourier, 'wave', split_axis=0, concat_axis=2, tiled=True)]
    pallas_call x1, Pallas kernels: 89.7 us -> 73.2 us  [zonal(): pl.pallas_call(zonal_kernel, out_shape=jax.ShapeDtypeStruct((2, lon, lat)...]
    all_to_all x1 -> x0, starting transfers between devices: 10.7 us -> none  [local(): lax.all_to_all(fourier, 'wave', split_axis=0, concat_axis=2, tiled=True)]
    select_n x3 -> x0, other arithmetic: 7.77 us -> none  [the longest x1 4.72 us: local(): jnp.where(alive_mask[None, None], spectral[0], jnp.zeros((), jnp.bfloat16))]
    transpose x0 -> x2, local copies, waits for them, and re-layouts: none -> 6.36 us  [the longest x1 6.29 us: local(): jnp.transpose(spectral[0], (2, 0, 1, 3))]
    reshape x2, local copies, waits for them, and re-layouts: 3 us -> 7.45 us  [the longest x1 6.64 us: local(): jnp.transpose(spectral[0], (2, 0, 1, 3))]
  transfers between devices with their start and end apart: 2 -> 0, of which waited for: 2 -> 0; matrix products, arithmetic and copies ran while one was open for 3% -> 0% of each run, Pallas kernels for 0% -> 0%
where the time goes in v3:
time: 148 us
  Pallas kernels  133 us (90%)
  local copies, waits for them, and re-layouts  15 us (10%)
    pallas_call x1, Pallas kernels, zonal(): pl.pallas_call(zonal_kernel, out_shape=jax.ShapeDtypeStruct((2, lon, lat)...  73.2 us
    pallas_call x1, Pallas kernels, spectral_part(): pl.pallas_call(spectral_kernel, out_shape=jax.ShapeDtypeStruct((chunks, p...  59.6 us
    reshape x1, local copies, waits for them, and re-layouts, local(): jnp.transpose(spectral[0], (2, 0, 1, 3))  6.64 us
    transpose x1, local copies, waits for them, and re-layouts, local(): jnp.transpose(spectral[0], (2, 0, 1, 3))  6.29 us

profile of v3, /device:TPU:1, one launch (start us, length us, event | category | flops | bytes accessed | tf_op | source)
XLA Modules:
  0.0 147.9 jit_solution(4837631631686902344)
XLA Ops:
  0.0 0.8 reshape.11
  0.8 0.1 copy.9
  0.9 0.1 broadcast_in_dim_reshape.3.wave_ref
  1.0 6.3 %copy.8 = bf16[10,128,2,640]{3,2,1,0:T(2,128)(2,1)} copy(bf16[10,128,2,640]{3,2,0,1:T(2,128)(2,1)} %bitcast.17) | data formatting | bytes 6553600 | tf_op jit(solution)/shard_map/transpose | solution.py:395
  7.3 0.0 copy-start.1
  7.3 0.0 copy-start.2
  7.3 6.6 %reshape.9.spec_ref = bf16[10,256,640]{2,1,0:T(8,128)(2,1)S(1)} reshape(bf16[10,128,2,640]{3,2,1,0:T(2,128)(2,1)} %copy.8) | data formatting | bytes 6553600 | tf_op jit(solution)/shard_map/reshape | solution.py:395
  13.9 0.0 copy-done.1
  13.9 0.0 copy-done.2
  13.9 0.0 copy-start
  13.9 1.1 copy-done
  15.1 0.0 copy-start.3
  15.1 0.0 copy-start.4
  15.1 59.6 %shard_map.64 = bf16[5,64,16,128]{3,2,1,0:T(8,128)(2,1)S(1)} custom-call(bf16[10,256,640]{2,1,0:T(8,128)(2,1)S(1)} %reshape.9.spec_ref, bf16[10,64,640]{2,1,0:T(8,128)(2,1)S(1)} %bitcast.13, s32[640]{0:T(1024)S(1)} %copy-done.1, s32[1,128]{1,0:T(1,128)S(1)} %bitcast.14), custom_call_target="tpu_custom_call" | custom-call | flops 838860800 | bytes 6291456 | tf_op jit(solution)/shard_map/pallas_call | solution.py:372
  74.6 0.0 copy-done.3
  74.7 0.0 copy-done.4
  74.7 73.2 %shard_map.65 = bf16[2,5136,256]{2,1,0:T(8,128)(2,1)} custom-call(bf16[5,1024,128]{2,1,0:T(8,128)(2,1)S(1)} %bitcast.12, s32[1,640]{1,0:T(1,128)S(1)} %broadcast_in_dim_reshape.3.wave_ref, s32[1,256]{1,0:T(1,128)S(1)} %bitcast.15, s32[1,256]{1,0:T(1,128)S(1)} %bitcast.16), custom_call_target="tpu_custom_call" | custom-call | flops 8053063680 | bytes 7340032 | tf_op jit(solution)/shard_map/pallas_call | solution.py:207
Async XLA Ops:
  7.3 6.7 %copy-start.1 = (s32[640]{0:T(1024)S(1)}, s32[640]{0:T(1024)}, u32[]{:S(2)}) copy-start(s32[640]{0:T(1024)} %wave_ref.1) | copy-start | bytes 7684
  7.3 6.7 %copy-start.2 = (s32[128]{0:T(128)S(1)}, s32[128]{0:T(128)}, u32[]{:S(2)}) copy-start(s32[128]{0:T(128)} %param.11) | copy-start | bytes 1540
  13.9 1.1 copy-start
  15.1 59.6 %copy-start.3 = (s32[256]{0:T(256)S(1)}, s32[256]{0:T(256)}, u32[]{:S(2)}) copy-start(s32[256]{0:T(256)} %param.9) | copy-start | bytes 3076
  15.1 59.6 %copy-start.4 = (s32[256]{0:T(256)S(1)}, s32[256]{0:T(256)}, u32[]{:S(2)}) copy-start(s32[256]{0:T(256)} %param.10) | copy-start | bytes 3076

commit v4 on v3

--- a/solution.py
+++ b/solution.py
@@ -83,20 +83,22 @@
             m = jnp.broadcast_to(wave_ref[:, t * LANES:(t + 1) * LANES].astype(f32), points.shape)
             weight = jnp.where(2.0 * m < points, jnp.where(m == 0.0, 1.0, 2.0), 0.0)
             half = turn(m, 2.0 * points, 0.5 * inverse)
-            steps = powers(turn(m * 8.0, points, inverse), 5)
+            near = powers(times(half, half), 9)
+            steps = powers(near[8], 5)
             for j, (c, s) in enumerate(steps):
                 step_c[t, pl.ds(j * 8, 8), :] = c
                 step_s[t, pl.ds(j * 8, 8), :] = s
             middle = times(half, steps[4])
-            for j, w in enumerate(powers(times(half, half), 8)):
+            for j, w in enumerate(near[:8]):
                 c, s = times(middle, w) if j else middle
                 inner_c[t, pl.ds(j * 8, 8), :] = c
                 inner_s[t, pl.ds(j * 8, 8), :] = s
             centre = times(times(steps[4], steps[4]), (half[0], -half[1]))
-            for j, (c, s) in enumerate(powers(turn(m * 128.0, points, inverse), 8)):
+            outer = powers(turn(m * 128.0, points, inverse), 9)
+            for j, (c, s) in enumerate(outer[:8]):
                 outer_c[t, pl.ds(j * 8, 8), :] = c
                 outer_s[t, pl.ds(j * 8, 8), :] = s
-            far = powers(turn(m * 1024.0, points, inverse), far_count)
+            far = powers(outer[8], far_count)
             for p in range(2):
                 value = (
                     live[2 * p, t, pl.ds(s0, SUBLANES), :] * weight,
@@ -234,7 +236,7 @@
 
 def spectral_kernel(
     spec_ref, leg_ref, wave_ref, field_ref, recv_ref,
-    legs, swap, mixed, outbox,
+    legs, swap, lefts, mixed, outbox,
     own_sem, send_a, recv_a, send_f, recv_f, send_m, recv_m, keep_m,
 ):
     bf16, f32 = jnp.bfloat16, jnp.float32
@@ -243,10 +245,11 @@
     right, left = lax.rem(y + 1, ring), lax.rem(y + ring - 1, ring)
     rows_here, lats_here, degrees = leg_ref.shape
     chunks = rows_here // 2
-    pairs = spec_ref.shape[1]
+    pairs = spec_ref.shape[0] * spec_ref.shape[2]
 
     def there(k):
-        return lax.rem(me + k, peers)
+        other = me + k
+        return jnp.where(other >= peers, other - peers, other)
 
     barrier = pltpu.get_barrier_semaphore()
 
@@ -256,7 +259,7 @@
 
     for side in (right, left):
         pl.semaphore_signal(barrier, inc=1, device_id=(me, side), device_id_type=MESH)
-    lax.fori_loop(1, peers, greet, 0)
+    lax.fori_loop(1, peers, greet, 0, unroll=9)
 
     def own():
         return pltpu.make_async_copy(leg_ref, legs.at[y], own_sem)
@@ -276,10 +279,11 @@
             device_id=(me, (right, left)[side]), device_id_type=MESH)
 
     def message(c, k):
+        other = there(k)
         return pltpu.make_async_remote_copy(
-            src_ref=outbox.at[c, there(k)], dst_ref=recv_ref.at[c, me],
+            src_ref=outbox.at[c, other], dst_ref=recv_ref.at[c, me],
             send_sem=send_m.at[c], recv_sem=recv_m.at[c],
-            device_id=(there(k), y), device_id_type=MESH)
+            device_id=(other, y), device_id_type=MESH)
 
     def all_messages(c):
         some = pl.ds(0, peers - 1)
@@ -306,7 +310,7 @@
 
     own().wait()
     pl.semaphore_wait(barrier, peers + 1)
-    for c in range(3):
+    for c in range(2):
         for side in range(2):
             first(c, side).start()
 
@@ -316,6 +320,11 @@
         for side in range(2):
             second(c, side).start()
 
+        @pl.when(c < chunks - 2)
+        def _():
+            for side in range(2):
+                first(c + 2, side).start()
+
     pass_on(0)
 
     def step(c, carry):
@@ -323,11 +332,8 @@
         def _():
             pass_on(c + 1)
 
-        @pl.when(c < chunks - 3)
-        def _():
-            for side in range(2):
-                first(c + 3, side).start()
-
+        for r in range(2):
+            lefts[r] = spec_ref[:, 2 * c + r].reshape(pairs, degrees)
         for side in range(2):
             second(c, side).wait_recv()
         degree = lax.broadcasted_iota(jnp.int32, (ring * lats_here, degrees), 1)
@@ -335,7 +341,7 @@
             row = 2 * c + r
             values = jnp.concatenate([legs[g, row] for g in range(ring)], axis=0)
             values = jnp.where(degree >= wave_ref[me * rows_here + row], values.astype(f32), 0.0).astype(bf16)
-            fourier = dot_nt(spec_ref[row], values).astype(bf16)
+            fourier = dot_nt(lefts[r], values).astype(bf16)
             fourier = jnp.dot(swap[...], fourier, preferred_element_type=f32)
             for h in range(2):
                 mixed[pl.ds(r * 2 + h, pairs, stride=4), :] = fourier[:, h * LANES:(h + 1) * LANES]
@@ -346,7 +352,7 @@
             message(c, k).start()
             return carry
 
-        return lax.fori_loop(1, peers, post, carry)
+        return lax.fori_loop(1, peers, post, carry, unroll=9)
 
     lax.fori_loop(0, chunks, step, 0)
 
@@ -362,7 +368,8 @@
 
 
 def spectral_part(spec, legendre, wave_of_row, field_slot, peers, ring):
-    rows_here, pairs, degrees = spec.shape
+    pairs, degrees = spec.shape[0] * spec.shape[2], spec.shape[3]
+    rows_here = spec.shape[1]
     lats_here = legendre.shape[1]
     chunks = rows_here // 2
     bf16 = jnp.bfloat16
@@ -377,6 +384,7 @@
         scratch_shapes=[
             pltpu.VMEM((ring, rows_here, lats_here, degrees), bf16),
             pltpu.VMEM((pairs, pairs), bf16),
+            pltpu.VMEM((2, pairs, degrees), bf16),
             pltpu.VMEM((peers * MESSAGE, LANES), jnp.float32),
             pltpu.VMEM((chunks, peers, MESSAGE, LANES), bf16),
             pltpu.SemaphoreType.DMA,
@@ -392,7 +400,7 @@
 def local(spectral, legendre, wave_of_row, row_points, lat_slot, field_slot):
     rows_here, degree_count, _ = legendre.shape
     peers, ring = lax.axis_size("wave"), lax.axis_size("fld")
-    spec = jnp.transpose(spectral[0], (2, 0, 1, 3)).reshape(rows_here, -1, degree_count)
+    spec = jnp.transpose(spectral[0], (0, 2, 1, 3))
     four = spectral_part(spec, jnp.transpose(legendre, (0, 2, 1)), wave_of_row, field_slot, peers, ring)
     four = four.reshape(rows_here // 2, peers * MESSAGE, LANES)
     waves = wave_of_row.reshape(peers, rows_here).T.reshape(-1)

time: 148 us -> 134 us (0.905)
  local copies, waits for them, and re-layouts: 15 us -> 5.43 us
  Pallas kernels: 133 us -> 128 us
    reshape x1 -> x0, local copies, waits for them, and re-layouts: 6.64 us -> none  [local(): jnp.transpose(spectral[0], (2, 0, 1, 3))]
    transpose x1 -> x0, local copies, waits for them, and re-layouts: 6.29 us -> none  [local(): jnp.transpose(spectral[0], (2, 0, 1, 3))]
    pallas_call x1, Pallas kernels: 59.6 us -> 56.1 us  [spectral_part(): pl.pallas_call(spectral_kernel, out_shape=jax.ShapeDtypeStruct((chunks, p...]
    unnamed x10 -> x12, local copies, waits for them, and re-layouts: 1.15 us -> 4.43 us
where the time goes in v4:
time: 134 us
  Pallas kernels  128 us (96%)
  local copies, waits for them, and re-layouts  5.43 us (4%)
    pallas_call x1, Pallas kernels, zonal(): pl.pallas_call(zonal_kernel, out_shape=jax.ShapeDtypeStruct((2, lon, lat)...  72 us
    pallas_call x1, Pallas kernels, spectral_part(): pl.pallas_call(spectral_kernel, out_shape=jax.ShapeDtypeStruct((chunks, p...  56.1 us
    unnamed x12, local copies, waits for them, and re-layouts  4.43 us

profile of v4, /device:TPU:1, one launch (start us, length us, event | category | flops | bytes accessed | tf_op | source)
XLA Modules:
  0.0 133.5 jit_solution(11357814177824427933)
XLA Ops:
  0.0 0.0 copy-start.5
  0.0 0.0 copy-start.4
  0.0 0.8 reshape.7
  0.8 0.1 copy.7
  0.9 0.1 broadcast_in_dim_reshape.3.wave_ref
  1.0 0.0 copy-start
  1.0 1.9 %copy-done = bf16[1,128,2,10,640]{4,2,3,1,0:T(2,128)(2,1)S(1)} copy-done((bf16[1,128,2,10,640]{4,2,3,1,0:T(2,128)(2,1)S(1)}, bf16[1,128,2,10,640]{4,2,3,1,0:T(2,128)(2,1)}, u32[]{:S(2)}) %copy-start) | copy-done | bytes 3276824
  2.9 0.0 copy-start.1
  2.9 1.1 copy-done.1
  4.1 0.0 copy-start.2
  4.1 0.7 copy-done.2
  4.8 0.0 copy-start.3
  4.8 0.7 copy-done.3
  5.4 56.1 %shard_map.64 = bf16[5,64,16,128]{3,2,1,0:T(8,128)(2,1)S(1)} custom-call(bf16[128,10,2,640]{3,2,1,0:T(2,128)(2,1)S(1)} %bitcast.12, bf16[10,64,640]{2,1,0:T(8,128)(2,1)S(1)} %bitcast.14, s32[640]{0:T(1024)S(1)} %copy-done.2, s32[1,128]{1,0:T(1,128)S(1)} %bitcast.15), custom_call_target="tpu_custom_call" | custom-call | flops 838860800 | bytes 6291456 | tf_op jit(solution)/shard_map/pallas_call | solution.py:379
  61.5 0.0 copy-done.5
  61.5 0.0 copy-done.4
  61.5 72.0 %shard_map.65 = bf16[2,5136,256]{2,1,0:T(8,128)(2,1)} custom-call(bf16[5,1024,128]{2,1,0:T(8,128)(2,1)S(1)} %bitcast.13, s32[1,640]{1,0:T(1,128)S(1)} %broadcast_in_dim_reshape.3.wave_ref, s32[1,256]{1,0:T(1,128)S(1)} %bitcast.16, s32[1,256]{1,0:T(1,128)S(1)} %bitcast.17), custom_call_target="tpu_custom_call" | custom-call | flops 8053063680 | bytes 7340032 | tf_op jit(solution)/shard_map/pallas_call | solution.py:209
Async XLA Ops:
  0.0 61.5 %copy-start.5 = (s32[256]{0:T(256)S(1)}, s32[256]{0:T(256)}, u32[]{:S(2)}) copy-start(s32[256]{0:T(256)} %param.10) | copy-start | bytes 3076
  0.0 61.5 %copy-start.4 = (s32[256]{0:T(256)S(1)}, s32[256]{0:T(256)}, u32[]{:S(2)}) copy-start(s32[256]{0:T(256)} %param.9) | copy-start | bytes 3076
  1.0 1.9 %copy-start = (bf16[1,128,2,10,640]{4,2,3,1,0:T(2,128)(2,1)S(1)}, bf16[1,128,2,10,640]{4,2,3,1,0:T(2,128)(2,1)}, u32[]{:S(2)}) copy-start(bf16[1,128,2,10,640]{4,2,3,1,0:T(2,128)(2,1)} %param.6) | copy-start | bytes 9830404
  2.9 1.1 copy-start.1
  4.1 0.7 copy-start.2
  4.8 0.7 copy-start.3

commit v5 on v4

--- a/solution.py
+++ b/solution.py
@@ -10,7 +10,9 @@
 
 LANES = 128
 SUBLANES = 8
+TOGETHER = 2
 MESSAGE = 16
+BUNDLES = ((0, 2), (2, 2), (4, 1))
 COARSE = 48
 
 
@@ -43,7 +45,7 @@
 
 def zonal_kernel(
     four_ref, wave_ref, points_ref, slot_ref, out_ref,
-    live, npts, place, wide, held, inner_c, inner_s, step_c, step_s, outer_c, outer_s, lead_r, lead_i, left, table, rows,
+    live, npts, place, wide, held, inner_c, inner_s, step_c, step_s, outer_c, outer_s, leap_c, leap_s, lead_r, lead_i, left, table, rows,
 ):
     lat = slot_ref.shape[1]
     waves = wave_ref.shape[1]
@@ -62,9 +64,9 @@
     order = order.astype(bf16)
     in_slot = jnp.where(row_i == slot_ref[...], 1.0, 0.0).astype(bf16)
     place[...] = jnp.dot(order, in_slot, preferred_element_type=f32).astype(bf16)
-    sources = four_ref.shape[1] // MESSAGE
-    for chunk in range(four_ref.shape[0]):
-        wide[...] = four_ref[chunk].astype(f32)
+    sources = four_ref.shape[0]
+    for chunk in range(four_ref.shape[1] // MESSAGE):
+        wide[...] = four_ref[:, pl.ds(chunk * MESSAGE, MESSAGE), :].astype(f32).reshape(wide.shape)
         for part in range(4):
             for r in range(2):
                 halves = [wide[pl.ds(part * 4 + r * 2 + h, sources, stride=MESSAGE), :] for h in range(2)]
@@ -75,7 +77,20 @@
         for t in range(tiles):
             live[part, t] = moved[:, t * LANES:(t + 1) * LANES]
 
-    def block(i, carry, far_count):
+    groups = SUBLANES // TOGETHER
+
+    def multiply(t0, buf, far_count):
+        count = 16 * far_count
+        used, half = pl.ds(0, TOGETHER * count), LANES // 2
+        even = dot_nt(left[buf, used, :waves], table[buf, :, :waves])
+        odd = dot_nt(left[buf, used, waves:], table[buf, :, waves:])
+        for l in range(TOGETHER):
+            e = even[l * count:(l + 1) * count, l * half:(l + 1) * half]
+            o = odd[l * count:(l + 1) * count, l * half:(l + 1) * half]
+            rows[pl.ds(t0 + l, count, stride=lat), :] = jnp.concatenate([e - o, e + o], axis=1)
+
+    def block(i, carry, far_count, first):
+        middle_step = far_count // 2 - 1
         s0 = pl.multiple_of(i * SUBLANES, SUBLANES)
         points = npts[pl.ds(s0, SUBLANES), :]
         inverse = 1.0 / points
@@ -98,19 +113,24 @@
             for j, (c, s) in enumerate(outer[:8]):
                 outer_c[t, pl.ds(j * 8, 8), :] = c
                 outer_s[t, pl.ds(j * 8, 8), :] = s
-            far = powers(outer[8], far_count)
+            far = powers(outer[8], far_count - middle_step)
+            for j, (c, s) in enumerate(far[1:]):
+                leap_c[t, pl.ds(j * 8, 8), :] = c
+                leap_s[t, pl.ds(j * 8, 8), :] = s
+            if middle_step:
+                centre = times(centre, far[middle_step])
             for p in range(2):
                 value = (
                     live[2 * p, t, pl.ds(s0, SUBLANES), :] * weight,
                     live[2 * p + 1, t, pl.ds(s0, SUBLANES), :] * weight,
                 )
-                value = times(value, centre)
-                for a, w in enumerate(far):
-                    r, im = times(value, w) if a else value
-                    lead_r[t, pl.ds((a * 2 + p) * 8, 8), :] = r
-                    lead_i[t, pl.ds((a * 2 + p) * 8, 8), :] = im
+                r, im = times(value, centre)
+                lead_r[t, pl.ds(p * 8, 8), :] = r
+                lead_i[t, pl.ds(p * 8, 8), :] = im
 
         def make(l, buf):
+            low, high = l % TOGETHER * (LANES // 2), l % TOGETHER * 16 * far_count
+
             def bcast(ref, t, row):
                 return ref[t, pl.ds(row * 8 + l, 8, stride=0), :]
 
@@ -130,32 +150,36 @@
                 here = pl.ds(t * LANES, LANES)
                 there = pl.ds(waves + t * LANES, LANES)
                 for q in range(4):
-                    table[buf, pl.ds(q * 16, 16), here] = jnp.concatenate(
+                    table[buf, pl.ds(low + q * 16, 16), here] = jnp.concatenate(
                         [cs[2 * q], cs[2 * q + 1]], axis=0).astype(bf16)
-                    table[buf, pl.ds(q * 16, 16), there] = jnp.concatenate(
+                    table[buf, pl.ds(low + q * 16, 16), there] = jnp.concatenate(
                         [ss[2 * q], ss[2 * q + 1]], axis=0).astype(bf16)
                 oc, os = spread(outer_c, t), spread(outer_s, t)
+                parts = [[None] * far_count for _ in range(2)]
+                for p in range(2):
+                    parts[p][middle_step] = times(
+                        (bcast(lead_r, t, p), bcast(lead_i, t, p)), (oc, os))
+                for j in range(1, far_count - middle_step):
+                    wc, ws = bcast(leap_c, t, j - 1), bcast(leap_s, t, j - 1)
+                    for p in range(2):
+                        r, im = parts[p][middle_step]
+                        a, b, c, d = r * wc, im * ws, im * wc, r * ws
+                        parts[p][middle_step + j] = (a - b, c + d)
+                        if j <= middle_step:
+                            parts[p][middle_step - j] = (a + b, c - d)
                 for q in range(far_count):
-                    res, ims = [], []
-                    for h in range(2):
-                        fr, fi = bcast(lead_r, t, 2 * q + h), bcast(lead_i, t, 2 * q + h)
-                        res.append(fr * oc - fi * os)
-                        ims.append(fr * os + fi * oc)
-                    left[buf, pl.ds(q * 16, 16), here] = jnp.concatenate(res, axis=0).astype(bf16)
-                    left[buf, pl.ds(q * 16, 16), there] = jnp.concatenate(ims, axis=0).astype(bf16)
-
-        def multiply(l, buf):
-            used = pl.ds(0, 16 * far_count)
-            even = dot_nt(left[buf, used, :waves], table[buf, :, :waves])
-            odd = dot_nt(left[buf, used, waves:], table[buf, :, waves:])
-            rows[pl.ds(s0 + l, 16 * far_count, stride=lat), :] = jnp.concatenate(
-                [even - odd, even + odd], axis=1)
-
-        make(0, 0)
-        for l in range(1, SUBLANES):
-            make(l, l % 2)
-            multiply(l - 1, (l - 1) % 2)
-        multiply(SUBLANES - 1, (SUBLANES - 1) % 2)
+                    for i, where in enumerate((here, there)):
+                        left[buf, pl.ds(high + q * 16, 16), where] = jnp.concatenate(
+                            [parts[0][q][i], parts[1][q][i]], axis=0).astype(bf16)
+
+        for g in range(groups):
+            for l in range(g * TOGETHER, (g + 1) * TOGETHER):
+                make(l, g % 2)
+            if g:
+                multiply(s0 + (g - 1) * TOGETHER, (g - 1) % 2, far_count)
+            else:
+                before = jnp.where(i > first, s0 - TOGETHER, s0 + SUBLANES - TOGETHER)
+                multiply(before, (groups - 1) % 2, far_count)
         return carry
 
     start = 0
@@ -165,7 +189,12 @@
         else:
             fits = jnp.where(count <= far_count * 1024.0, 1.0, 0.0)
             end = jnp.sum(fits).astype(jnp.int32) // SUBLANES
-        lax.fori_loop(start, end, functools.partial(block, far_count=far_count), 0)
+        lax.fori_loop(start, end, functools.partial(block, far_count=far_count, first=start), 0)
+
+        @pl.when(end > start)
+        def _(end=end, far_count=far_count):
+            multiply(end * SUBLANES - TOGETHER, (groups - 1) % 2, far_count)
+
         start = end
 
     def longitude_of(shape):
@@ -215,12 +244,12 @@
             pltpu.VMEM((4, tiles, lat, LANES), f32),
             pltpu.VMEM((lat, LANES), f32),
             pltpu.VMEM((lat, lat), jnp.bfloat16),
-            pltpu.VMEM(four.shape[1:], f32),
+            pltpu.VMEM((four.shape[0] * MESSAGE, LANES), f32),
             pltpu.VMEM((4, waves, lat), jnp.bfloat16),
             scratch(8), scratch(8), scratch(5), scratch(5), scratch(8), scratch(8),
-            scratch(2 * COARSE // 8), scratch(2 * COARSE // 8),
-            pltpu.VMEM((2, 2 * COARSE, 2 * waves), jnp.bfloat16),
-            pltpu.VMEM((2, LANES // 2, 2 * waves), jnp.bfloat16),
+            scratch(COARSE // 16), scratch(COARSE // 16), scratch(2), scratch(2),
+            pltpu.VMEM((2, TOGETHER * 2 * COARSE, 2 * waves), jnp.bfloat16),
+            pltpu.VMEM((2, TOGETHER * LANES // 2, 2 * waves), jnp.bfloat16),
             pltpu.VMEM((2 * COARSE * lat, LANES), f32),
         ],
         compiler_params=pltpu.CompilerParams(vmem_limit_bytes=48 * 1024 * 1024),
@@ -235,9 +264,9 @@
 
 
 def spectral_kernel(
-    spec_ref, leg_ref, wave_ref, field_ref, recv_ref,
-    legs, swap, lefts, mixed, outbox,
-    own_sem, send_a, recv_a, send_f, recv_f, send_m, recv_m, keep_m,
+    spec_hbm, leg_ref, wave_ref, field_ref, recv_ref,
+    spec_ref, legs, swap, lefts, mixed, outbox,
+    spec_sem, own_sem, send_a, recv_a, send_f, recv_f, send_m, recv_m, keep_m,
 ):
     bf16, f32 = jnp.bfloat16, jnp.float32
     me, y = lax.axis_index("wave"), lax.axis_index("fld")
@@ -278,23 +307,30 @@
             send_sem=send_f.at[side, c], recv_sem=recv_f.at[side, c],
             device_id=(me, (right, left)[side]), device_id_type=MESH)
 
-    def message(c, k):
+    def rows_of(g):
+        return pl.ds(BUNDLES[g][0] * MESSAGE, BUNDLES[g][1] * MESSAGE)
+
+    def message(g, k):
         other = there(k)
         return pltpu.make_async_remote_copy(
-            src_ref=outbox.at[c, other], dst_ref=recv_ref.at[c, me],
-            send_sem=send_m.at[c], recv_sem=recv_m.at[c],
+            src_ref=outbox.at[other, rows_of(g)], dst_ref=recv_ref.at[me, rows_of(g)],
+            send_sem=send_m.at[g], recv_sem=recv_m.at[g],
             device_id=(other, y), device_id_type=MESH)
 
-    def all_messages(c):
+    def all_messages(g):
         some = pl.ds(0, peers - 1)
         return pltpu.make_async_remote_copy(
-            src_ref=outbox.at[c, some], dst_ref=recv_ref.at[c, some],
-            send_sem=send_m.at[c], recv_sem=recv_m.at[c],
+            src_ref=outbox.at[some, rows_of(g)], dst_ref=recv_ref.at[some, rows_of(g)],
+            send_sem=send_m.at[g], recv_sem=recv_m.at[g],
             device_id=(there(1), y), device_id_type=MESH)
 
-    def kept(c):
-        return pltpu.make_async_copy(outbox.at[c, me], recv_ref.at[c, me], keep_m.at[c])
-
+    def kept(g):
+        return pltpu.make_async_copy(outbox.at[me, rows_of(g)], recv_ref.at[me, rows_of(g)], keep_m.at[g])
+
+    def spec_copy():
+        return pltpu.make_async_copy(spec_hbm, spec_ref, spec_sem)
+
+    spec_copy().start()
     own().start()
 
     row_i = lax.broadcasted_iota(jnp.int32, (pairs, pairs), 0)
@@ -313,6 +349,7 @@
     for c in range(2):
         for side in range(2):
             first(c, side).start()
+    spec_copy().wait()
 
     def pass_on(c):
         for side in range(2):
@@ -345,26 +382,30 @@
             fourier = jnp.dot(swap[...], fourier, preferred_element_type=f32)
             for h in range(2):
                 mixed[pl.ds(r * 2 + h, pairs, stride=4), :] = fourier[:, h * LANES:(h + 1) * LANES]
-        outbox[c] = mixed[...].astype(bf16).reshape(outbox.shape[1:])
-        kept(c).start()
-
-        def post(k, carry):
-            message(c, k).start()
+        outbox[:, pl.ds(pl.multiple_of(c * MESSAGE, MESSAGE), MESSAGE), :] = mixed[...].astype(bf16).reshape(
+            peers, MESSAGE, LANES)
+        return carry
+
+    for g, (c0, size) in enumerate(BUNDLES):
+        lax.fori_loop(c0, c0 + size, step, 0)
+        kept(g).start()
+
+        def post(k, carry, g=g):
+            message(g, k).start()
             return carry
 
-        return lax.fori_loop(1, peers, post, carry, unroll=9)
-
-    lax.fori_loop(0, chunks, step, 0)
+        lax.fori_loop(1, peers, post, 0, unroll=9)
 
     def finish(c, carry):
         for side in range(2):
             first(c, side).wait_send()
             second(c, side).wait_send()
-        kept(c).wait()
-        all_messages(c).wait()
         return carry
 
     lax.fori_loop(0, chunks, finish, 0)
+    for g in range(len(BUNDLES)):
+        kept(g).wait()
+        all_messages(g).wait()
 
 
 def spectral_part(spec, legendre, wave_of_row, field_slot, peers, ring):
@@ -374,21 +415,24 @@
     chunks = rows_here // 2
     bf16 = jnp.bfloat16
     vmem = pl.BlockSpec(memory_space=pltpu.VMEM)
+    hbm = pl.BlockSpec(memory_space=pltpu.HBM)
     pairs_sem = pltpu.SemaphoreType.DMA((2, chunks))
-    chunk_sem = pltpu.SemaphoreType.DMA((chunks,))
+    bundle_sem = pltpu.SemaphoreType.DMA((len(BUNDLES),))
     return pl.pallas_call(
         spectral_kernel,
-        out_shape=jax.ShapeDtypeStruct((chunks, peers, MESSAGE, LANES), bf16),
-        in_specs=[vmem, vmem, pl.BlockSpec(memory_space=pltpu.SMEM), vmem],
+        out_shape=jax.ShapeDtypeStruct((peers, chunks * MESSAGE, LANES), bf16),
+        in_specs=[hbm, hbm, pl.BlockSpec(memory_space=pltpu.SMEM), vmem],
         out_specs=pl.BlockSpec(memory_space=pl.ANY),
         scratch_shapes=[
+            pltpu.VMEM(spec.shape, bf16),
             pltpu.VMEM((ring, rows_here, lats_here, degrees), bf16),
             pltpu.VMEM((pairs, pairs), bf16),
             pltpu.VMEM((2, pairs, degrees), bf16),
             pltpu.VMEM((peers * MESSAGE, LANES), jnp.float32),
-            pltpu.VMEM((chunks, peers, MESSAGE, LANES), bf16),
+            pltpu.VMEM((peers, chunks * MESSAGE, LANES), bf16),
             pltpu.SemaphoreType.DMA,
-            pairs_sem, pairs_sem, pairs_sem, pairs_sem, chunk_sem, chunk_sem, chunk_sem,
+            pltpu.SemaphoreType.DMA,
+            pairs_sem, pairs_sem, pairs_sem, pairs_sem, bundle_sem, bundle_sem, bundle_sem,
         ],
         compiler_params=pltpu.CompilerParams(
             collective_id=0, has_side_effects=True, vmem_limit_bytes=40 * 1024 * 1024),
@@ -402,7 +446,6 @@
     peers, ring = lax.axis_size("wave"), lax.axis_size("fld")
     spec = jnp.transpose(spectral[0], (0, 2, 1, 3))
     four = spectral_part(spec, jnp.transpose(legendre, (0, 2, 1)), wave_of_row, field_slot, peers, ring)
-    four = four.reshape(rows_here // 2, peers * MESSAGE, LANES)
     waves = wave_of_row.reshape(peers, rows_here).T.reshape(-1)
     grid = zonal(four, waves, row_points, lat_slot, LON)
     return jnp.transpose(grid, (0, 2, 1))[None]

time: 134 us -> 138 us (1.030)
  Pallas kernels: 128 us -> 132 us
    pallas_call x1, Pallas kernels: 56.1 us -> 61.3 us  [spectral_part(): pl.pallas_call(spectral_kernel, out_shape=jax.ShapeDtypeStruct((peers, ch...]
    pallas_call x1, Pallas kernels: 72 us -> 70.6 us  [zonal(): pl.pallas_call(zonal_kernel, out_shape=jax.ShapeDtypeStruct((2, lon, lat)...]
where the time goes in v5:
time: 138 us; the launch traced here: 137 us
  Pallas kernels  132 us (96%)
  local copies, waits for them, and re-layouts  5.43 us (4%)
    pallas_call x1, Pallas kernels, zonal(): pl.pallas_call(zonal_kernel, out_shape=jax.ShapeDtypeStruct((2, lon, lat)...  70.6 us
    pallas_call x1, Pallas kernels, spectral_part(): pl.pallas_call(spectral_kernel, out_shape=jax.ShapeDtypeStruct((peers, ch...  61.3 us
    unnamed x12, local copies, waits for them, and re-layouts  4.43 us

profile of v5, /device:TPU:1, one launch (start us, length us, event | category | flops | bytes accessed | tf_op | source)
XLA Modules:
  0.0 137.3 jit_solution(4495974342476953853)
XLA Ops:
  0.0 0.0 copy-start.5
  0.0 0.0 copy-start.4
  0.0 0.8 reshape.3
  0.8 0.1 copy.7
  0.9 0.1 broadcast_in_dim_reshape.3.wave_ref
  1.0 0.0 copy-start
  1.0 1.9 %copy-done = bf16[1,128,2,10,640]{4,2,3,1,0:T(2,128)(2,1)S(1)} copy-done((bf16[1,128,2,10,640]{4,2,3,1,0:T(2,128)(2,1)S(1)}, bf16[1,128,2,10,640]{4,2,3,1,0:T(2,128)(2,1)}, u32[]{:S(2)}) %copy-start) | copy-done | bytes 3276824
  2.9 0.0 copy-start.1
  2.9 1.1 copy-done.1
  4.1 0.0 copy-start.2
  4.1 0.7 copy-done.2
  4.8 0.0 copy-start.3
  4.8 0.7 copy-done.3
  5.4 61.3 %shard_map.64.four_ref = bf16[64,80,128]{2,1,0:T(8,128)(2,1)S(1)} custom-call(bf16[128,10,2,640]{3,2,1,0:T(2,128)(2,1)S(1)} %bitcast.11, bf16[10,64,640]{2,1,0:T(8,128)(2,1)S(1)} %bitcast.12, s32[640]{0:T(1024)S(1)} %copy-done.2, s32[1,128]{1,0:T(1,128)S(1)} %bitcast.13), custom_call_target="tpu_custom_call" | custom-call | flops 838860800 | bytes 6291456 | tf_op jit(solution)/shard_map/pallas_call | solution.py:421
  66.7 0.0 copy-done.5
  66.7 0.0 copy-done.4
  66.7 70.6 %shard_map.65 = bf16[2,5136,256]{2,1,0:T(8,128)(2,1)} custom-call(bf16[64,80,128]{2,1,0:T(8,128)(2,1)S(1)} %shard_map.64.four_ref, s32[1,640]{1,0:T(1,128)S(1)} %broadcast_in_dim_reshape.3.wave_ref, s32[1,256]{1,0:T(1,128)S(1)} %bitcast.14, s32[1,256]{1,0:T(1,128)S(1)} %bitcast.15), custom_call_target="tpu_custom_call" | custom-call | flops 8053063680 | bytes 7340032 | tf_op jit(solution)/shard_map/pallas_call | solution.py:238
Async XLA Ops:
  0.0 66.7 %copy-start.5 = (s32[256]{0:T(256)S(1)}, s32[256]{0:T(256)}, u32[]{:S(2)}) copy-start(s32[256]{0:T(256)} %param.10) | copy-start | bytes 3076
  0.0 66.7 %copy-start.4 = (s32[256]{0:T(256)S(1)}, s32[256]{0:T(256)}, u32[]{:S(2)}) copy-start(s32[256]{0:T(256)} %param.9) | copy-start | bytes 3076
  1.0 1.9 %copy-start = (bf16[1,128,2,10,640]{4,2,3,1,0:T(2,128)(2,1)S(1)}, bf16[1,128,2,10,640]{4,2,3,1,0:T(2,128)(2,1)}, u32[]{:S(2)}) copy-start(bf16[1,128,2,10,640]{4,2,3,1,0:T(2,128)(2,1)} %param.6) | copy-start | bytes 9830404
  2.9 1.1 copy-start.1
  4.1 0.7 copy-start.2
  4.8 0.7 copy-start.3

commit v6 on v5

--- a/solution.py
+++ b/solution.py
@@ -12,7 +12,7 @@
 SUBLANES = 8
 TOGETHER = 2
 MESSAGE = 16
-BUNDLES = ((0, 2), (2, 2), (4, 1))
+BUNDLES = tuple((c, 1) for c in range(5))
 COARSE = 48
 
 
@@ -45,7 +45,7 @@
 
 def zonal_kernel(
     four_ref, wave_ref, points_ref, slot_ref, out_ref,
-    live, npts, place, wide, held, inner_c, inner_s, step_c, step_s, outer_c, outer_s, leap_c, leap_s, lead_r, lead_i, left, table, rows,
+    live, npts, place, wide, held, inner_c, inner_s, step_c, step_s, outer_c, outer_s, leap_c, leap_s, lead_r, lead_i, left_a, left_b, table_a, table_b, rows,
 ):
     lat = slot_ref.shape[1]
     waves = wave_ref.shape[1]
@@ -53,6 +53,7 @@
     lon = out_ref.shape[1]
     blocks = pl.cdiv(lon, LANES)
     bf16, f32 = jnp.bfloat16, jnp.float32
+    left, table = (left_a, left_b), (table_a, table_b)
 
     row_i = lax.broadcasted_iota(jnp.int32, (lat, lat), 0)
     eye = jnp.where(row_i == lax.broadcasted_iota(jnp.int32, (lat, lat), 1), 1.0, 0.0)
@@ -82,8 +83,8 @@
     def multiply(t0, buf, far_count):
         count = 16 * far_count
         used, half = pl.ds(0, TOGETHER * count), LANES // 2
-        even = dot_nt(left[buf, used, :waves], table[buf, :, :waves])
-        odd = dot_nt(left[buf, used, waves:], table[buf, :, waves:])
+        even = dot_nt(left[buf][used, :waves], table[buf][:, :waves])
+        odd = dot_nt(left[buf][used, waves:], table[buf][:, waves:])
         for l in range(TOGETHER):
             e = even[l * count:(l + 1) * count, l * half:(l + 1) * half]
             o = odd[l * count:(l + 1) * count, l * half:(l + 1) * half]
@@ -150,9 +151,9 @@
                 here = pl.ds(t * LANES, LANES)
                 there = pl.ds(waves + t * LANES, LANES)
                 for q in range(4):
-                    table[buf, pl.ds(low + q * 16, 16), here] = jnp.concatenate(
+                    table[buf][pl.ds(low + q * 16, 16), here] = jnp.concatenate(
                         [cs[2 * q], cs[2 * q + 1]], axis=0).astype(bf16)
-                    table[buf, pl.ds(low + q * 16, 16), there] = jnp.concatenate(
+                    table[buf][pl.ds(low + q * 16, 16), there] = jnp.concatenate(
                         [ss[2 * q], ss[2 * q + 1]], axis=0).astype(bf16)
                 oc, os = spread(outer_c, t), spread(outer_s, t)
                 parts = [[None] * far_count for _ in range(2)]
@@ -169,7 +170,7 @@
                             parts[p][middle_step - j] = (a + b, c - d)
                 for q in range(far_count):
                     for i, where in enumerate((here, there)):
-                        left[buf, pl.ds(high + q * 16, 16), where] = jnp.concatenate(
+                        left[buf][pl.ds(high + q * 16, 16), where] = jnp.concatenate(
                             [parts[0][q][i], parts[1][q][i]], axis=0).astype(bf16)
 
         for g in range(groups):
@@ -231,6 +232,9 @@
     tiles = waves // LANES
     f32 = jnp.float32
     vmem = pl.BlockSpec(memory_space=pltpu.VMEM)
+
+    left_shape = pltpu.VMEM((TOGETHER * 2 * COARSE, 2 * waves), jnp.bfloat16)
+    table_shape = pltpu.VMEM((TOGETHER * LANES // 2, 2 * waves), jnp.bfloat16)
 
     def scratch(count):
         return pltpu.VMEM((tiles, count * 8, LANES), f32)
@@ -248,8 +252,7 @@
             pltpu.VMEM((4, waves, lat), jnp.bfloat16),
             scratch(8), scratch(8), scratch(5), scratch(5), scratch(8), scratch(8),
             scratch(COARSE // 16), scratch(COARSE // 16), scratch(2), scratch(2),
-            pltpu.VMEM((2, TOGETHER * 2 * COARSE, 2 * waves), jnp.bfloat16),
-            pltpu.VMEM((2, TOGETHER * LANES // 2, 2 * waves), jnp.bfloat16),
+            left_shape, left_shape, table_shape, table_shape,
             pltpu.VMEM((2 * COARSE * lat, LANES), f32),
         ],
         compiler_params=pltpu.CompilerParams(vmem_limit_bytes=48 * 1024 * 1024),
@@ -346,9 +349,8 @@
 
     own().wait()
     pl.semaphore_wait(barrier, peers + 1)
-    for c in range(2):
-        for side in range(2):
-            first(c, side).start()
+    for side in range(2):
+        first(0, side).start()
     spec_copy().wait()
 
     def pass_on(c):
@@ -357,10 +359,10 @@
         for side in range(2):
             second(c, side).start()
 
-        @pl.when(c < chunks - 2)
+        @pl.when(c < chunks - 1)
         def _():
             for side in range(2):
-                first(c + 2, side).start()
+                first(c + 1, side).start()
 
     pass_on(0)
 
@@ -435,7 +437,7 @@
             pairs_sem, pairs_sem, pairs_sem, pairs_sem, bundle_sem, bundle_sem, bundle_sem,
         ],
         compiler_params=pltpu.CompilerParams(
-            collective_id=0, has_side_effects=True, vmem_limit_bytes=40 * 1024 * 1024),
+            collective_id=0, has_side_effects=True, vmem_limit_bytes=60 * 1024 * 1024),
         cost_estimate=pl.CostEstimate(
             flops=2 * rows_here * pairs * degrees * lats_here * ring, bytes_accessed=6 << 20, transcendentals=0),
     )(spec, legendre, wave_of_row, field_slot[None])

time: 138 us -> 133 us (0.964)
  local copies, waits for them, and re-layouts: 5.43 us -> 2.31 us
  Pallas kernels: 132 us -> 130 us
    unnamed x12 -> x6, local copies, waits for them, and re-layouts: 4.43 us -> 1.32 us
    pallas_call x1, Pallas kernels: 61.3 us -> 59.7 us  [spectral_part(): pl.pallas_call(spectral_kernel, out_shape=jax.ShapeDtypeStruct((peers, ch...]
where the time goes in v6:
time: 133 us
  Pallas kernels  130 us (98%)
  local copies, waits for them, and re-layouts  2.31 us (2%)
    pallas_call x1, Pallas kernels, zonal(): pl.pallas_call(zonal_kernel, out_shape=jax.ShapeDtypeStruct((2, lon, lat)...  70.6 us
    pallas_call x1, Pallas kernels, spectral_part(): pl.pallas_call(spectral_kernel, out_shape=jax.ShapeDtypeStruct((peers, ch...  59.7 us

profile of v6, /device:TPU:1, one launch (start us, length us, event | category | flops | bytes accessed | tf_op | source)
XLA Modules:
  0.0 132.6 jit_solution(10656032393864782566)
XLA Ops:
  0.0 0.0 copy-start.2
  0.0 0.0 copy-start.1
  0.0 0.8 reshape.3
  0.8 0.1 copy.7
  0.9 0.1 broadcast_in_dim_reshape.3.wave_ref
  1.0 59.7 %shard_map.64.four_ref = bf16[64,80,128]{2,1,0:T(8,128)(2,1)} custom-call(bf16[128,10,2,640]{3,2,1,0:T(2,128)(2,1)} %bitcast.13, bf16[10,64,640]{2,1,0:T(8,128)(2,1)} %bitcast.14, s32[640]{0:T(1024)} %wave_ref.1, s32[1,128]{1,0:T(1,128)} %bitcast.16), custom_call_target="tpu_custom_call" | custom-call | flops 838860800 | bytes 6291456 | tf_op jit(solution)/shard_map/pallas_call | solution.py:423
  60.7 0.0 copy-done.2
  60.7 0.0 copy-done.1
  60.7 0.0 copy-start
  60.7 1.3 copy-done
  62.0 70.6 %shard_map.65 = bf16[2,5136,256]{2,1,0:T(8,128)(2,1)} custom-call(bf16[64,80,128]{2,1,0:T(8,128)(2,1)S(1)} %copy-done, s32[1,640]{1,0:T(1,128)S(1)} %broadcast_in_dim_reshape.3.wave_ref, s32[1,256]{1,0:T(1,128)S(1)} %bitcast.11, s32[1,256]{1,0:T(1,128)S(1)} %bitcast.12), custom_call_target="tpu_custom_call" | custom-call | flops 8053063680 | bytes 7340032 | tf_op jit(solution)/shard_map/pallas_call | solution.py:242
Async XLA Ops:
  0.0 60.7 %copy-start.2 = (s32[256]{0:T(256)S(1)}, s32[256]{0:T(256)}, u32[]{:S(2)}) copy-start(s32[256]{0:T(256)} %param.10) | copy-start | bytes 3076
  0.0 60.7 %copy-start.1 = (s32[256]{0:T(256)S(1)}, s32[256]{0:T(256)}, u32[]{:S(2)}) copy-start(s32[256]{0:T(256)} %param.9) | copy-start | bytes 3076
  60.7 1.3 copy-start

commit v7 on v6

--- a/solution.py
+++ b/solution.py
@@ -10,6 +10,8 @@
 
 LANES = 128
 SUBLANES = 8
+STEP = 5
+PAD = 8
 TOGETHER = 2
 MESSAGE = 16
 BUNDLES = tuple((c, 1) for c in range(5))
@@ -88,7 +90,7 @@
         for l in range(TOGETHER):
             e = even[l * count:(l + 1) * count, l * half:(l + 1) * half]
             o = odd[l * count:(l + 1) * count, l * half:(l + 1) * half]
-            rows[pl.ds(t0 + l, count, stride=lat), :] = jnp.concatenate([e - o, e + o], axis=1)
+            rows[pl.ds(t0 + l, count, stride=lat + PAD), :] = jnp.concatenate([e - o, e + o], axis=1)
 
     def block(i, carry, far_count, first):
         middle_step = far_count // 2 - 1
@@ -204,27 +206,28 @@
 
     square = (LANES, LANES)
     small = jnp.where(lax.broadcasted_iota(jnp.int32, square, 0) == longitude_of(square), 1.0, 0.0).astype(bf16)
-    lane = longitude_of((lat, LANES)).astype(f32)
+    npts[...] = npts[...] - longitude_of((lat, LANES)).astype(f32)
 
     def turned(p, a):
         at = (a // 8) * 16 + p * 8 + a % 8
-        value = rows[pl.ds(pl.multiple_of(at * lat, lat), lat), :]
+        value = rows[pl.ds(pl.multiple_of(at * (lat + PAD), 8), lat), :]
         first = jnp.float32(a * LANES) if isinstance(a, int) else (a * LANES).astype(f32)
-        value = jnp.where(lane + first < npts[...], value, 0.0).astype(bf16)
-        value = dot_nt(small, value).astype(bf16)
-        return jnp.dot(value, place[...], preferred_element_type=f32).astype(bf16)
-
+        return dot_nt(small, jnp.where(npts[...] > first, value, 0.0).astype(bf16)).astype(bf16)
+
+    def placed(values):
+        return jnp.dot(jnp.concatenate(values, axis=0), place[...], preferred_element_type=f32).astype(bf16)
+
+    whole_blocks = lon // LANES
     for p in range(2):
-        def whole(h, carry, p=p):
-            for a in (2 * h, 2 * h + 1):
-                out_ref[p, pl.ds(pl.multiple_of(a * LANES, LANES), LANES), :] = turned(p, a)
+        def some(h, carry, p=p):
+            out_ref[p, pl.ds(pl.multiple_of(h * STEP * LANES, LANES), STEP * LANES), :] = placed(
+                [turned(p, h * STEP + i) for i in range(STEP)])
             return carry
 
-        lax.fori_loop(0, (blocks - 1) // 2, whole, 0)
-        for a in range((blocks - 1) // 2 * 2, blocks):
-            first = a * LANES
-            size = min(LANES, lon - first)
-            out_ref[p, first:first + size, :] = turned(p, a)[:size]
+        lax.fori_loop(0, whole_blocks // STEP, some, 0)
+        for a in range(whole_blocks // STEP * STEP, blocks):
+            size = min(LANES, lon - a * LANES)
+            out_ref[p, a * LANES:a * LANES + size, :] = placed([turned(p, a)])[:size]
 
 
 def zonal(four, wave_of_row, row_points, lat_slot, lon):
@@ -253,7 +256,7 @@
             scratch(8), scratch(8), scratch(5), scratch(5), scratch(8), scratch(8),
             scratch(COARSE // 16), scratch(COARSE // 16), scratch(2), scratch(2),
             left_shape, left_shape, table_shape, table_shape,
-            pltpu.VMEM((2 * COARSE * lat, LANES), f32),
+            pltpu.VMEM((2 * COARSE * (lat + PAD), LANES), f32),
         ],
         compiler_params=pltpu.CompilerParams(vmem_limit_bytes=48 * 1024 * 1024),
         cost_estimate=pl.CostEstimate(
@@ -392,11 +395,14 @@
         lax.fori_loop(c0, c0 + size, step, 0)
         kept(g).start()
 
+        message(g, peers // 2).start()
+
         def post(k, carry, g=g):
-            message(g, k).start()
+            message(g, peers // 2 - k).start()
+            message(g, peers // 2 + k).start()
             return carry
 
-        lax.fori_loop(1, peers, post, 0, unroll=9)
+        lax.fori_loop(1, peers // 2, post, 0, unroll=4)
 
     def finish(c, carry):
         for side in range(2):

time: 133 us -> 122 us (0.917)
  Pallas kernels: 130 us -> 120 us
    pallas_call x1, Pallas kernels: 70.6 us -> 60.1 us  [zonal(): pl.pallas_call(zonal_kernel, out_shape=jax.ShapeDtypeStruct((2, lon, lat)...]
where the time goes in v7:
time: 122 us
  Pallas kernels  120 us (98%)
  local copies, waits for them, and re-layouts  2.31 us (2%)
    pallas_call x1, Pallas kernels, zonal(): pl.pallas_call(zonal_kernel, out_shape=jax.ShapeDtypeStruct((2, lon, lat)...  60.1 us
    pallas_call x1, Pallas kernels, spectral_part(): pl.pallas_call(spectral_kernel, out_shape=jax.ShapeDtypeStruct((peers, ch...  59.8 us

profile of v7, /device:TPU:1, one launch (start us, length us, event | category | flops | bytes accessed | tf_op | source)
XLA Modules:
  0.0 122.2 jit_solution(7111146976722271624)
XLA Ops:
  0.0 0.0 copy-start.2
  0.0 0.0 copy-start.1
  0.0 0.8 reshape.3
  0.8 0.1 copy.7
  0.9 0.1 broadcast_in_dim_reshape.3.wave_ref
  1.0 59.8 %shard_map.64.four_ref = bf16[64,80,128]{2,1,0:T(8,128)(2,1)} custom-call(bf16[128,10,2,640]{3,2,1,0:T(2,128)(2,1)} %bitcast.13, bf16[10,64,640]{2,1,0:T(8,128)(2,1)} %bitcast.14, s32[640]{0:T(1024)} %wave_ref.1, s32[1,128]{1,0:T(1,128)} %bitcast.16), custom_call_target="tpu_custom_call" | custom-call | flops 838860800 | bytes 6291456 | tf_op jit(solution)/shard_map/pallas_call | solution.py:429
  60.8 0.0 copy-done.2
  60.8 0.0 copy-done.1
  60.8 0.0 copy-start
  60.8 1.3 %copy-done = bf16[64,80,128]{2,1,0:T(8,128)(2,1)S(1)} copy-done((bf16[64,80,128]{2,1,0:T(8,128)(2,1)S(1)}, bf16[64,80,128]{2,1,0:T(8,128)(2,1)}, u32[]{:S(2)}) %copy-start) | copy-done | bytes 1310744
  62.2 60.1 %shard_map.65 = bf16[2,5136,256]{2,1,0:T(8,128)(2,1)} custom-call(bf16[64,80,128]{2,1,0:T(8,128)(2,1)S(1)} %copy-done, s32[1,640]{1,0:T(1,128)S(1)} %broadcast_in_dim_reshape.3.wave_ref, s32[1,256]{1,0:T(1,128)S(1)} %bitcast.11, s32[1,256]{1,0:T(1,128)S(1)} %bitcast.12), custom_call_target="tpu_custom_call" | custom-call | flops 8053063680 | bytes 7340032 | tf_op jit(solution)/shard_map/pallas_call | solution.py:245
Async XLA Ops:
  0.0 60.8 %copy-start.2 = (s32[256]{0:T(256)S(1)}, s32[256]{0:T(256)}, u32[]{:S(2)}) copy-start(s32[256]{0:T(256)} %param.10) | copy-start | bytes 3076
  0.0 60.8 %copy-start.1 = (s32[256]{0:T(256)S(1)}, s32[256]{0:T(256)}, u32[]{:S(2)}) copy-start(s32[256]{0:T(256)} %param.9) | copy-start | bytes 3076
  60.8 1.3 %copy-start = (bf16[64,80,128]{2,1,0:T(8,128)(2,1)S(1)}, bf16[64,80,128]{2,1,0:T(8,128)(2,1)}, u32[]{:S(2)}) copy-start(bf16[64,80,128]{2,1,0:T(8,128)(2,1)} %shard_map.64.four_ref) | copy-start | bytes 3932164

commit v8 on v7

--- a/solution.py
+++ b/solution.py
@@ -14,6 +14,7 @@
 PAD = 8
 TOGETHER = 2
 MESSAGE = 16
+EARLY = 6
 BUNDLES = tuple((c, 1) for c in range(5))
 COARSE = 48
 
@@ -92,9 +93,9 @@
             o = odd[l * count:(l + 1) * count, l * half:(l + 1) * half]
             rows[pl.ds(t0 + l, count, stride=lat + PAD), :] = jnp.concatenate([e - o, e + o], axis=1)
 
-    def block(i, carry, far_count, first):
+    def phases(i, far_count):
         middle_step = far_count // 2 - 1
-        s0 = pl.multiple_of(i * SUBLANES, SUBLANES)
+        s0 = pl.multiple_of(jnp.minimum(i, lat // SUBLANES - 1) * SUBLANES, SUBLANES)
         points = npts[pl.ds(s0, SUBLANES), :]
         inverse = 1.0 / points
         for t in range(tiles):
@@ -131,6 +132,10 @@
                 lead_r[t, pl.ds(p * 8, 8), :] = r
                 lead_i[t, pl.ds(p * 8, 8), :] = im
 
+    def block(i, carry, far_count, first):
+        middle_step = far_count // 2 - 1
+        s0 = pl.multiple_of(i * SUBLANES, SUBLANES)
+
         def make(l, buf):
             low, high = l % TOGETHER * (LANES // 2), l % TOGETHER * 16 * far_count
 
@@ -183,15 +188,17 @@
             else:
                 before = jnp.where(i > first, s0 - TOGETHER, s0 + SUBLANES - TOGETHER)
                 multiply(before, (groups - 1) % 2, far_count)
-        return carry
-
-    start = 0
+        phases(i + 1, far_count)
+        return carry
+
+    start = jnp.int32(0)
     for far_count in range(2, COARSE // 8 + 1, 2):
         if far_count == COARSE // 8:
             end = lat // SUBLANES
         else:
             fits = jnp.where(count <= far_count * 1024.0, 1.0, 0.0)
             end = jnp.sum(fits).astype(jnp.int32) // SUBLANES
+        phases(start, far_count)
         lax.fori_loop(start, end, functools.partial(block, far_count=far_count, first=start), 0)
 
         @pl.when(end > start)
@@ -218,13 +225,15 @@
         return jnp.dot(jnp.concatenate(values, axis=0), place[...], preferred_element_type=f32).astype(bf16)
 
     whole_blocks = lon // LANES
-    for p in range(2):
-        def some(h, carry, p=p):
+
+    def some(h, carry):
+        for p in range(2):
             out_ref[p, pl.ds(pl.multiple_of(h * STEP * LANES, LANES), STEP * LANES), :] = placed(
                 [turned(p, h * STEP + i) for i in range(STEP)])
-            return carry
-
-        lax.fori_loop(0, whole_blocks // STEP, some, 0)
+        return carry
+
+    lax.fori_loop(0, whole_blocks // STEP, some, 0)
+    for p in range(2):
         for a in range(whole_blocks // STEP * STEP, blocks):
             size = min(LANES, lon - a * LANES)
             out_ref[p, a * LANES:a * LANES + size, :] = placed([turned(p, a)])[:size]
@@ -350,11 +359,17 @@
     wanted = wanted + (col_i[0:1] % 2).astype(f32)
     swap[...] = dot_nt(eye, jnp.where(row_i.astype(f32) == wanted, 1.0, 0.0).astype(bf16)).astype(bf16)
 
+    def regroup(row, carry):
+        lefts[row] = jnp.dot(
+            swap[...], spec_ref[:, row].reshape(pairs, degrees), preferred_element_type=f32).astype(bf16)
+        return carry
+
+    spec_copy().wait()
+    lax.fori_loop(0, 2, regroup, 0)
     own().wait()
     pl.semaphore_wait(barrier, peers + 1)
     for side in range(2):
         first(0, side).start()
-    spec_copy().wait()
 
     def pass_on(c):
         for side in range(2):
@@ -367,6 +382,7 @@
             for side in range(2):
                 first(c + 1, side).start()
 
+    lax.fori_loop(2, EARLY, regroup, 0)
     pass_on(0)
 
     def step(c, carry):
@@ -374,17 +390,14 @@
         def _():
             pass_on(c + 1)
 
-        for r in range(2):
-            lefts[r] = spec_ref[:, 2 * c + r].reshape(pairs, degrees)
         for side in range(2):
             second(c, side).wait_recv()
-        degree = lax.broadcasted_iota(jnp.int32, (ring * lats_here, degrees), 1)
+        degree = lax.broadcasted_iota(jnp.int32, (1, degrees), 1)
         for r in range(2):
             row = 2 * c + r
             values = jnp.concatenate([legs[g, row] for g in range(ring)], axis=0)
-            values = jnp.where(degree >= wave_ref[me * rows_here + row], values.astype(f32), 0.0).astype(bf16)
-            fourier = dot_nt(lefts[r], values).astype(bf16)
-            fourier = jnp.dot(swap[...], fourier, preferred_element_type=f32)
+            keep = jnp.where(degree >= wave_ref[me * rows_here + row], 1.0, 0.0).astype(bf16)
+            fourier = dot_nt(lefts[row], values * keep)
             for h in range(2):
                 mixed[pl.ds(r * 2 + h, pairs, stride=4), :] = fourier[:, h * LANES:(h + 1) * LANES]
         outbox[:, pl.ds(pl.multiple_of(c * MESSAGE, MESSAGE), MESSAGE), :] = mixed[...].astype(bf16).reshape(
@@ -403,6 +416,8 @@
             return carry
 
         lax.fori_loop(1, peers // 2, post, 0, unroll=4)
+        row = EARLY + 2 * g
+        lax.fori_loop(min(row, rows_here), min(row + 2, rows_here), regroup, 0)
 
     def finish(c, carry):
         for side in range(2):
@@ -435,7 +450,7 @@
             pltpu.VMEM(spec.shape, bf16),
             pltpu.VMEM((ring, rows_here, lats_here, degrees), bf16),
             pltpu.VMEM((pairs, pairs), bf16),
-            pltpu.VMEM((2, pairs, degrees), bf16),
+            pltpu.VMEM((rows_here, pairs, degrees), bf16),
             pltpu.VMEM((peers * MESSAGE, LANES), jnp.float32),
             pltpu.VMEM((peers, chunks * MESSAGE, LANES), bf16),
             pltpu.SemaphoreType.DMA,

time: 122 us -> 121 us (level)
  no operation moved by 1% of the time
where the time goes in v8:
time: 121 us
  Pallas kernels  119 us (98%)
  local copies, waits for them, and re-layouts  2.31 us (2%)
    pallas_call x1, Pallas kernels, zonal(): pl.pallas_call(zonal_kernel, out_shape=jax.ShapeDtypeStruct((2, lon, lat)...  59.4 us
    pallas_call x1, Pallas kernels, spectral_part(): pl.pallas_call(spectral_kernel, out_shape=jax.ShapeDtypeStruct((peers, ch...  59.3 us

profile of v8, /device:TPU:1, one launch (start us, length us, event | category | flops | bytes accessed | tf_op | source)
XLA Modules:
  0.0 121.0 jit_solution(16865446203464257796)
XLA Ops:
  0.0 0.0 copy-start.2
  0.0 0.0 copy-start.1
  0.0 0.8 reshape.3
  0.8 0.1 copy.7
  0.9 0.1 broadcast_in_dim_reshape.3.wave_ref
  1.0 59.3 %shard_map.64.four_ref = bf16[64,80,128]{2,1,0:T(8,128)(2,1)} custom-call(bf16[128,10,2,640]{3,2,1,0:T(2,128)(2,1)} %bitcast.13, bf16[10,64,640]{2,1,0:T(8,128)(2,1)} %bitcast.14, s32[640]{0:T(1024)} %wave_ref.1, s32[1,128]{1,0:T(1,128)} %bitcast.16), custom_call_target="tpu_custom_call" | custom-call | flops 838860800 | bytes 6291456 | tf_op jit(solution)/shard_map/pallas_call | solution.py:444
  60.3 0.0 copy-done.2
  60.3 0.0 copy-done.1
  60.3 0.0 copy-start
  60.3 1.3 %copy-done = bf16[64,80,128]{2,1,0:T(8,128)(2,1)S(1)} copy-done((bf16[64,80,128]{2,1,0:T(8,128)(2,1)S(1)}, bf16[64,80,128]{2,1,0:T(8,128)(2,1)}, u32[]{:S(2)}) %copy-start) | copy-done | bytes 1310744
  61.6 59.4 %shard_map.65 = bf16[2,5136,256]{2,1,0:T(8,128)(2,1)} custom-call(bf16[64,80,128]{2,1,0:T(8,128)(2,1)S(1)} %copy-done, s32[1,640]{1,0:T(1,128)S(1)} %broadcast_in_dim_reshape.3.wave_ref, s32[1,256]{1,0:T(1,128)S(1)} %bitcast.11, s32[1,256]{1,0:T(1,128)S(1)} %bitcast.12), custom_call_target="tpu_custom_call" | custom-call | flops 8053063680 | bytes 7340032 | tf_op jit(solution)/shard_map/pallas_call | solution.py:254
Async XLA Ops:
  0.0 60.3 %copy-start.2 = (s32[256]{0:T(256)S(1)}, s32[256]{0:T(256)}, u32[]{:S(2)}) copy-start(s32[256]{0:T(256)} %param.10) | copy-start | bytes 3076
  0.0 60.3 %copy-start.1 = (s32[256]{0:T(256)S(1)}, s32[256]{0:T(256)}, u32[]{:S(2)}) copy-start(s32[256]{0:T(256)} %param.9) | copy-start | bytes 3076
  60.3 1.3 %copy-start = (bf16[64,80,128]{2,1,0:T(8,128)(2,1)S(1)}, bf16[64,80,128]{2,1,0:T(8,128)(2,1)}, u32[]{:S(2)}) copy-start(bf16[64,80,128]{2,1,0:T(8,128)(2,1)} %shard_map.64.four_ref) | copy-start | bytes 3932164

commit v9 on v8

--- a/solution.py
+++ b/solution.py
@@ -94,7 +94,7 @@
             rows[pl.ds(t0 + l, count, stride=lat + PAD), :] = jnp.concatenate([e - o, e + o], axis=1)
 
     def phases(i, far_count):
-        middle_step = far_count // 2 - 1
+        middle_step = (far_count - 1) // 2
         s0 = pl.multiple_of(jnp.minimum(i, lat // SUBLANES - 1) * SUBLANES, SUBLANES)
         points = npts[pl.ds(s0, SUBLANES), :]
         inverse = 1.0 / points
@@ -133,7 +133,7 @@
                 lead_i[t, pl.ds(p * 8, 8), :] = im
 
     def block(i, carry, far_count, first):
-        middle_step = far_count // 2 - 1
+        middle_step = (far_count - 1) // 2
         s0 = pl.multiple_of(i * SUBLANES, SUBLANES)
 
         def make(l, buf):
@@ -192,7 +192,7 @@
         return carry
 
     start = jnp.int32(0)
-    for far_count in range(2, COARSE // 8 + 1, 2):
+    for far_count in range(1, COARSE // 8 + 1):
         if far_count == COARSE // 8:
             end = lat // SUBLANES
         else:
@@ -368,8 +368,9 @@
     lax.fori_loop(0, 2, regroup, 0)
     own().wait()
     pl.semaphore_wait(barrier, peers + 1)
-    for side in range(2):
-        first(0, side).start()
+    for c in range(2):
+        for side in range(2):
+            first(c, side).start()
 
     def pass_on(c):
         for side in range(2):
@@ -377,10 +378,10 @@
         for side in range(2):
             second(c, side).start()
 
-        @pl.when(c < chunks - 1)
+        @pl.when(c < chunks - 2)
         def _():
             for side in range(2):
-                first(c + 1, side).start()
+                first(c + 2, side).start()
 
     lax.fori_loop(2, EARLY, regroup, 0)
     pass_on(0)

time: 121 us -> 116 us (0.959)
  Pallas kernels: 119 us -> 114 us
    pallas_call x1, Pallas kernels: 59.3 us -> 56.2 us  [spectral_part(): pl.pallas_call(spectral_kernel, out_shape=jax.ShapeDtypeStruct((peers, ch...]
    pallas_call x1, Pallas kernels: 59.4 us -> 57.8 us  [zonal(): pl.pallas_call(zonal_kernel, out_shape=jax.ShapeDtypeStruct((2, lon, lat)...]
where the time goes in v9:
time: 116 us
  Pallas kernels  114 us (98%)
  local copies, waits for them, and re-layouts  2.31 us (2%)
    pallas_call x1, Pallas kernels, zonal(): pl.pallas_call(zonal_kernel, out_shape=jax.ShapeDtypeStruct((2, lon, lat)...  57.8 us
    pallas_call x1, Pallas kernels, spectral_part(): pl.pallas_call(spectral_kernel, out_shape=jax.ShapeDtypeStruct((peers, ch...  56.2 us

profile of v9, /device:TPU:1, one launch (start us, length us, event | category | flops | bytes accessed | tf_op | source)
XLA Modules:
  0.0 116.3 jit_solution(2073326101931679944)
XLA Ops:
  0.0 0.0 copy-start.2
  0.0 0.0 copy-start.1
  0.0 0.8 reshape.3
  0.8 0.1 copy.7
  0.9 0.1 broadcast_in_dim_reshape.3.wave_ref
  1.0 56.2 %shard_map.64.four_ref = bf16[64,80,128]{2,1,0:T(8,128)(2,1)} custom-call(bf16[128,10,2,640]{3,2,1,0:T(2,128)(2,1)} %bitcast.13, bf16[10,64,640]{2,1,0:T(8,128)(2,1)} %bitcast.14, s32[640]{0:T(1024)} %wave_ref.1, s32[1,128]{1,0:T(1,128)} %bitcast.16), custom_call_target="tpu_custom_call" | custom-call | flops 838860800 | bytes 6291456 | tf_op jit(solution)/shard_map/pallas_call | solution.py:445
  57.2 0.0 copy-done.2
  57.2 0.0 copy-done.1
  57.2 0.0 copy-start
  57.2 1.3 %copy-done = bf16[64,80,128]{2,1,0:T(8,128)(2,1)S(1)} copy-done((bf16[64,80,128]{2,1,0:T(8,128)(2,1)S(1)}, bf16[64,80,128]{2,1,0:T(8,128)(2,1)}, u32[]{:S(2)}) %copy-start) | copy-done | bytes 1310744
  58.5 57.8 %shard_map.65 = bf16[2,5136,256]{2,1,0:T(8,128)(2,1)} custom-call(bf16[64,80,128]{2,1,0:T(8,128)(2,1)S(1)} %copy-done, s32[1,640]{1,0:T(1,128)S(1)} %broadcast_in_dim_reshape.3.wave_ref, s32[1,256]{1,0:T(1,128)S(1)} %bitcast.11, s32[1,256]{1,0:T(1,128)S(1)} %bitcast.12), custom_call_target="tpu_custom_call" | custom-call | flops 8053063680 | bytes 7340032 | tf_op jit(solution)/shard_map/pallas_call | solution.py:254
Async XLA Ops:
  0.0 57.2 %copy-start.2 = (s32[256]{0:T(256)S(1)}, s32[256]{0:T(256)}, u32[]{:S(2)}) copy-start(s32[256]{0:T(256)} %param.10) | copy-start | bytes 3076
  0.0 57.2 %copy-start.1 = (s32[256]{0:T(256)S(1)}, s32[256]{0:T(256)}, u32[]{:S(2)}) copy-start(s32[256]{0:T(256)} %param.9) | copy-start | bytes 3076
  57.2 1.3 %copy-start = (bf16[64,80,128]{2,1,0:T(8,128)(2,1)S(1)}, bf16[64,80,128]{2,1,0:T(8,128)(2,1)}, u32[]{:S(2)}) copy-start(bf16[64,80,128]{2,1,0:T(8,128)(2,1)} %shard_map.64.four_ref) | copy-start | bytes 3932164
